TPU v7x, 32 devices: a whole 2x2x4 slice. The times are simulated.
32 devices in a mesh: dp: 4 (over y, x), tensor: 8 (over z, core).
Axes of the slice: x: 2, y: 2, z: 4, core: 2. Of those that a mesh axis runs over, the one named last changes fastest.
Arguments:
- tokens: bfloat16 [4096, 4096], P(('dp', 'tensor')), may hold values from -6 to 6
- panel: bfloat16 [4096, 1024], P('tensor'), may hold values from -0.09375 to 0.09375
- cotangent: bfloat16 [4096, 512], P(('dp', 'tensor')), may hold values from -6 to 6
Outputs:
- hidden: float32 [4096, 512], P(('dp', 'tensor'))
- grad_panel: float32 [4096, 1024], P('tensor')
All inputs are finite; a program needn't handle non-finite values.
Results may differ from a plain program's by a relative error of at most 0.015.
Values may be sent and summed in bfloat16 or wider, within the bound.
A program may use at most 64 MiB of HBM per device.

v0:
```python
import math

import jax
import jax.numpy as jnp
from jax import lax
from jax.sharding import PartitionSpec as P


def grad_rows(token_block, grad_block, scale):
    product = lax.dot_general(
        token_block, grad_block, (((0,), (0,)), ((), ())), preferred_element_type=jnp.float32
    )
    return product * scale


def on_device(tokens, panel, cotangent):
    tok_rows, in_width = tokens.shape
    n_tensor = lax.axis_size("tensor")
    n_replica = lax.axis_size("dp")
    panel_cols = panel.shape[1]
    hidden_units = panel_cols // 2
    scale = 1.0 / math.sqrt(tok_rows * n_tensor * n_replica)
    projected = jnp.dot(
        tokens,
        lax.all_gather(panel, "tensor", axis=0, tiled=True),
        preferred_element_type=jnp.float32,
    )
    gate_pre = projected[:, :hidden_units]
    up_pre = projected[:, hidden_units:]
    sigmoid_gate = jax.nn.sigmoid(gate_pre)
    hidden = gate_pre * sigmoid_gate * up_pre
    grad_out = cotangent.astype(jnp.float32)
    gate_grad = grad_out * up_pre * sigmoid_gate * (1.0 + gate_pre * (1.0 - sigmoid_gate))
    up_grad = grad_out * gate_pre * sigmoid_gate
    pre_grad = jnp.concatenate([gate_grad, up_grad], axis=1).astype(jnp.bfloat16)
    owned = lax.psum_scatter(
        grad_rows(tokens, pre_grad, scale).astype(jnp.bfloat16),
        "tensor",
        scatter_dimension=0,
        tiled=True,
    ).astype(jnp.float32)
    grad_panel = lax.psum(owned, "dp")
    return (hidden, grad_panel)


def solution(mesh):
    placed = (P(("dp", "tensor"), None), P("tensor", None), P(("dp", "tensor"), None))
    return jax.shard_map(
        on_device,
        mesh=mesh,
        in_specs=placed,
        out_specs=(P(("dp", "tensor"), None), P("tensor", None)),
        check_vma=False,
    )
```

profile of v0, /device:TPU:24, one launch (start us, length us, event | category | flops | bytes accessed | tf_op | source)
XLA Modules:
  0.0 273.4 jit_solution(1918427513358259283)
XLA Ops:
  7.2 0.0 copy-start
  7.2 0.0 all-gather.2.cloned.1.call-start
  7.2 0.7 all-gather.2.cloned.1.call-update
  7.9 0.0 copy-start.1
  7.9 0.0 reduce-scatter.2.cloned.1.call-start
  8.0 82.0 %all-gather.2.cloned.1.call-done = bf16[4096,1024]{1,0:T(8,128)(2,1)} async-done(((bf16[512,1024]{1,0:T(8,128)(2,1)}), bf16[4096,1024]{1,0:T(8,128)(2,1)}) %all-gather.2.cloned.1.call-update) | async-done | bytes 8388624 | tf_op jit(solution)/shard_map/all_gather | solution.py:25
  90.0 0.0 copy-done
  90.0 4.6 %fusion.10 = f32[128,1024]{1,0:T(8,128)S(1)} fusion(bf16[128,4096]{1,0:T(8,128)(2,1)S(1)} %copy-done, bf16[4096,1024]{1,0:T(8,128)(2,1)} %all-gather.2.cloned.1.call-done), kind=kOutput, calls=%fused_computation.15 | convolution fusion | flops 1073741824 | bytes 9961472 | tf_op jit(solution)/shard_map/dot_general | solution.py:23
  94.6 0.0 copy-done.1
  94.6 0.9 fusion.3
  95.5 5.6 %fusion = bf16[4096,1024]{0,1:T(8,128)(2,1)} fusion(bf16[128,4096]{1,0:T(8,128)(2,1)S(1)} %copy-done, bf16[128,512]{1,0:T(8,128)(2,1)S(1)} %get-tuple-element.5, bf16[128,512]{1,0:T(8,128)(2,1)S(1)} %get-tuple-element.4), kind=kOutput, calls=%fused_computation.1 | convolution fusion | flops 1082654720 | bytes 9699328 | tf_op jit(solution)/shard_map/dot_general | solution.py:10
  101.1 0.0 reduce-scatter.2.cloned.1.call-update
  101.1 88.5 %reduce-scatter.2.cloned.1.call-done = bf16[512,1024]{0,1:T(8,128)(2,1)} async-done(((bf16[4096,1024]{0,1:T(8,128)(2,1)}), bf16[512,1024]{0,1:T(8,128)(2,1)}) %reduce-scatter.2.cloned.1.call-update) | async-done | bytes 1048592 | tf_op jit(solution)/shard_map/reduce_scatter | solution.py:36
  189.6 75.2 %all-reduce.1 = f32[512,1024]{0,1:T(8,128)S(1)} all-reduce(bf16[512,1024]{0,1:T(8,128)(2,1)} %reduce-scatter.2.cloned.1.call-done), channel_id=1, replica_groups=mesh['dp'=4,'tensor'=8] {'dp'}, use_global_device_ids=true, to_apply=%region_1.0 | all-reduce | flops 524288 | bytes 3145728 | tf_op jit(solution)/shard_map/psum | solution.py:42
  264.8 1.8 copy.5
Async XLA Ops:
  7.2 82.8 %copy-start = (bf16[128,4096]{1,0:T(8,128)(2,1)S(1)}, bf16[128,4096]{1,0:T(8,128)(2,1)}, u32[]{:S(2)}) copy-start(bf16[128,4096]{1,0:T(8,128)(2,1)} %param.3) | copy-start | bytes 3145732
  7.2 82.8 %all-gather.2.cloned.1.call-start = ((), (), s32[]{:S(2)}) async-start(), calls=%async_computation.1 | async-start | bytes 9437184 | tf_op jit(solution)/shard_map/all_gather | solution.py:25
  7.9 86.7 %copy-start.1 = (bf16[128,512]{1,0:T(8,128)(2,1)S(1)}, bf16[128,512]{1,0:T(8,128)(2,1)}, u32[]{:S(2)}) copy-start(bf16[128,512]{1,0:T(8,128)(2,1)} %param.5) | copy-start | bytes 393220
  7.9 181.6 %reduce-scatter.2.cloned.1.call-start = ((), (), s32[]{:S(2)}) async-start(), calls=%async_computation.2 | async-start | bytes 9437184 | tf_op jit(solution)/shard_map/reduce_scatter | solution.py:36
Sparse Core Ops, SparseCore 0:
  9.6 80.2 all-gather.1
  101.2 88.3 reduce-scatter.1
where the time goes:
time: 276 us; the launch traced here: 273 us
  waiting for transfers between devices  171 us (62%)
  blocking collectives  75.2 us (27%)
  between operations  14.1 us (5%)
  matrix products  10.2 us (4%)
    reduce_scatter x1, waiting for transfers between devices, on_device(): lax.psum_scatter(grad_rows(tokens, pre_grad, scale).astype(jnp.bfloat16),...  88.5 us
    all_gather x1, waiting for transfers between devices, on_device(): lax.all_gather(panel, 'tensor', axis=0, tiled=True)  82 us
    psum x1, blocking collectives, on_device(): grad_panel = lax.psum(owned, 'dp')  75.2 us
    dot_general x1, matrix products, grad_rows(): lax.dot_general(token_block, grad_block, (((0,), (0,)), ((), ())), prefer...  5.6 us
  transfers between devices with their start and end apart: 2, of which 2 were waited for; matrix products, arithmetic and copies ran while one was open for 0% of the time, Pallas kernels for 0%

commit v1 on v0

v1 whole, which is shorter than its diff:
```python
import functools
import math

import jax
import jax.numpy as jnp
from jax import lax
from jax.experimental import pallas as pl
from jax.experimental.pallas import tpu as pltpu
from jax.sharding import PartitionSpec as P

MESH = pl.DeviceIdType.MESH
PARTS = 2


def repeat(low, high, body):
    if high - low <= 4:
        for i in range(low, high):
            body(i)
    else:
        lax.fori_loop(low, high, lambda i, carry: (body(i), carry)[1], 0)


def factor(n):
    return max(f for f in range(1, math.isqrt(n) + 1) if n % f == 0)


def kernel(
    n_dp, n_tensor, scale,
    tokens, panel, cotangent,
    hidden, grad,
    full, tok_all, tok_t, pre_all, acc, out_part, in_part,
    f1_s, f1_r, row_s, row_r, col_s, col_r, d0_s, d0_r, d1_s, d1_r, sib_s, sib_r,
    tok_s, tok_r, pre_s, pre_r, pair_s, pair_r, rs_s, rs_r, ag_s, ag_r,
):
    n_tok, _ = tokens.shape
    depth, cols = panel.shape
    units = cols // 2
    width = cols // PARTS
    n_z = n_tensor // 2
    n_b = factor(n_dp)
    n_a = n_dp // n_b
    d, t = lax.axis_index("dp"), lax.axis_index("tensor")
    a, b = d // n_b, d % n_b
    z, c = t // 2, t % 2
    pair = z * 2 + 1 - c

    chunk_rows = max(16, depth // n_dp)
    down = depth // chunk_rows
    across = n_dp // down

    def chunk(i, span, half=None):
        wide = span // across
        row = pl.multiple_of((i // across) * chunk_rows, chunk_rows)
        start = (i % across) * wide
        if half is not None:
            wide = wide // 2
            start = start + half * wide
        return pl.ds(row, chunk_rows), pl.ds(pl.multiple_of(start, wide), wide)

    def send(src, dst, s, r, dp, tensor):
        return pltpu.make_async_remote_copy(
            src_ref=src, dst_ref=dst, send_sem=s, recv_sem=r,
            device_id=(dp, tensor), device_id_type=MESH,
        )

    def blk(k):
        return ((z - k + n_z) % n_z) * 2 + c

    def far(k, core):
        return ((z + k) % n_z) * 2 + core

    def f1(k, src_blk=None):
        where = chunk(d, cols)
        own = t if src_blk is None else src_blk
        return send(panel.at[where], full.at[(own,) + where], f1_s.at[k], f1_r.at[k], d, far(k, c))

    def piece(k, i, s, r, to, half=None):
        ref = full.at[(blk(k),) + chunk(i, cols, half)]
        return send(ref, ref, s.at[k], r.at[k], to, t)

    def a_peer(i):
        return ((a + i + n_a) % n_a) * n_b + b

    def b_peer(j):
        return a * n_b + (b + j + n_b) % n_b

    def ab_peer(i, j):
        return ((a + i + n_a) % n_a) * n_b + (b + j + n_b) % n_b

    def sib(k):
        src = panel if isinstance(k, int) and k == 0 else full.at[blk(k)]
        return send(src, full.at[blk(k)], sib_s.at[k], sib_r.at[k], d, pair)

    def tok(k, other):
        to = far(k, (1 - c) if other else c)
        src = tokens.at[:, pl.ds(pl.multiple_of(to * depth, depth), depth)]
        return send(src, tok_all.at[t], tok_s.at[k, other], tok_r.at[k, other], d, to)

    def rows_of(i):
        return pl.ds(pl.multiple_of(i * n_tok, n_tok), n_tok)

    def pre(h, k, own):
        ref = pre_all.at[h, rows_of(own)]
        return send(ref, ref, pre_s.at[h, k], pre_r.at[h, k], d, far(k, c))

    def pre_pair(h, k):
        ref = pre_all.at[h, rows_of(blk(k))]
        return send(ref, ref, pair_s.at[h, k], pair_r.at[h, k], d, pair)

    def rs(h, j):
        to = (d + j) % n_dp
        return send(out_part.at[h, to], in_part.at[h, j], rs_s.at[h, j], rs_r.at[h, j], to, t)

    def place(h, i):
        row, col = chunk(i, width)
        return row, pl.ds(pl.multiple_of(h * width + col.start, col.size), col.size)

    def ag(h, j, i):
        ref = grad.at[place(h, i)]
        return send(ref, ref, ag_s.at[h, j], ag_r.at[h, j], (d + j) % n_dp, t)

    barrier = pltpu.get_barrier_semaphore()

    def greet_tensor(k):
        pl.semaphore_signal(barrier, inc=1, device_id=(d, (t + k) % n_tensor), device_id_type=MESH)

    def greet_dp(k):
        pl.semaphore_signal(barrier, inc=1, device_id=((d + k) % n_dp, t), device_id_type=MESH)

    repeat(1, n_tensor, greet_tensor)
    repeat(1, n_dp, greet_dp)
    pl.semaphore_wait(barrier, n_tensor + n_dp - 2)

    repeat(1, n_z, lambda k: f1(k).start())
    sib(0).start()
    tok(0, 1).start()

    def multiply(own, ref):
        x = tokens[:, pl.ds(pl.multiple_of(own * depth, depth), depth)]
        return jnp.dot(x, ref[...], preferred_element_type=jnp.float32)

    acc[...] = multiply(t, panel)

    def spread(k):
        f1(k, blk(k)).wait_recv()
        repeat(1, n_b, lambda j: piece(k, d, row_s, row_r, b_peer(j)).start())
        repeat(1, n_a, lambda i: piece(k, d, col_s, col_r, a_peer(i)).start())
        tok(k, 0).start()
        tok(k, 1).start()

    def relay(k):
        repeat(1, n_b, lambda j: piece(k, b_peer(-j), row_s, row_r, d).wait_recv())

        def pass_a(j):
            repeat(1, n_a, lambda i: piece(k, b_peer(-j), d0_s, d0_r, a_peer(i), 0).start())

        repeat(1, n_b, pass_a)
        repeat(1, n_a, lambda i: piece(k, a_peer(-i), col_s, col_r, d).wait_recv())

        def pass_b(i):
            repeat(1, n_b, lambda j: piece(k, a_peer(-i), d1_s, d1_r, b_peer(j), 1).start())

        repeat(1, n_a, pass_b)

    def finish(k):
        def corner(i):
            def corner_b(j):
                piece(k, ab_peer(-i, -j), d0_s, d0_r, d, 0).wait_recv()
                piece(k, ab_peer(-i, -j), d1_s, d1_r, d, 1).wait_recv()
            repeat(1, n_b, corner_b)
        repeat(1, n_a, corner)
        sib(k).start()
        acc[...] += multiply(blk(k), full.at[blk(k)])

    def other(k):
        own = ((z - k + n_z) % n_z) * 2 + 1 - c
        dst = full.at[own]
        send(dst, dst, sib_s.at[k], sib_r.at[k], d, pair).wait_recv()
        acc[...] += multiply(own, dst)

    def when(k, body):
        if isinstance(k, int):
            if 1 <= k < n_z:
                body(k)
        else:
            pl.when((k >= 1) & (k < n_z))(lambda: body(k))

    def stage(k):
        when(k, spread)
        when(k - 1, relay)
        when(k - 2, finish)
        when(k - 3, other)

    for k in range(1, min(n_z, 4)):
        stage(k)
        if k == 1:
            other(0)
    if n_z > 4:
        lax.fori_loop(4, n_z, lambda k, carry: (stage(k), carry)[1], 0)
    for k in range(n_z, n_z + 3):
        stage(k)

    gate = acc[:, :units]
    up = acc[:, units:]
    s = jax.nn.sigmoid(gate)
    act = gate * s
    hidden[...] = act * up
    ct = cotangent[...].astype(jnp.float32)
    gate_grad = ct * up * s * (1.0 + gate * (1.0 - s))
    pre_all[0, rows_of(t), :] = gate_grad.astype(jnp.bfloat16)
    pre_all[1, rows_of(t), :] = (ct * act).astype(jnp.bfloat16)

    for h in range(PARTS):
        repeat(1, n_z, lambda k: pre(h, k, t).start())
        pre_pair(h, 0).start()

    tok_t[:, rows_of(t)] = tokens[:, pl.ds(pl.multiple_of(t * depth, depth), depth)].T

    def take(own, k, index):
        dst = tok_all.at[own]
        send(dst, dst, tok_s.at[k, index], tok_r.at[k, index], d, pair).wait_recv()
        tok_t[:, rows_of(own)] = dst[...].T

    take(pair, 0, 1)

    def take_both(k):
        take(blk(k), k, 0)
        take(((z - k + n_z) % n_z) * 2 + 1 - c, k, 1)

    repeat(1, n_z, take_both)

    def reduced(h):
        repeat(1, n_dp, lambda j: rs(h, j).wait_recv())
        total = out_part[h, d].astype(jnp.float32)
        for j in range(1, n_dp):
            total = total + in_part[h, j].astype(jnp.float32)
        grad[place(h, d)] = total.astype(jnp.bfloat16)
        repeat(1, n_dp, lambda j: ag(h, j, d).start())

    for h in range(PARTS):
        def arrive(k):
            pre(h, k, blk(k)).wait_recv()
            pre_pair(h, k).start()

        def arrive_pair(k):
            own = ((z - k + n_z) % n_z) * 2 + 1 - c
            ref = pre_all.at[h, rows_of(own)]
            send(ref, ref, pair_s.at[h, k], pair_r.at[h, k], d, pair).wait_recv()

        repeat(1, n_z, arrive)
        repeat(0, n_z, arrive_pair)
        def product(i):
            row, col = chunk(i, width)
            term = jnp.dot(tok_t[row, :], pre_all[h, :, col], preferred_element_type=jnp.float32)
            out_part[h, i] = (term * scale).astype(jnp.bfloat16)

        repeat(0, n_dp, product)
        repeat(1, n_dp, lambda j: rs(h, j).start())
        reduced(h)

    for h in range(PARTS):
        repeat(1, n_dp, lambda j: ag(h, j, (d - j + n_dp) % n_dp).wait_recv())

    def sent(k):
        f1(k).wait_send()
        repeat(1, n_b, lambda j: piece(k, d, row_s, row_r, b_peer(j)).wait_send())
        repeat(1, n_a, lambda i: piece(k, d, col_s, col_r, a_peer(i)).wait_send())

        def corner(i):
            def corner_b(j):
                piece(k, b_peer(-j), d0_s, d0_r, a_peer(i), 0).wait_send()
                piece(k, a_peer(-i), d1_s, d1_r, b_peer(j), 1).wait_send()
            repeat(1, n_b, corner_b)
        repeat(1, n_a, corner)
        sib(k).wait_send()
        tok(k, 0).wait_send()
        tok(k, 1).wait_send()
        for h in range(PARTS):
            pre(h, k, t).wait_send()
            pre_pair(h, k).wait_send()

    repeat(1, n_z, sent)
    sib(0).wait_send()
    tok(0, 1).wait_send()
    for h in range(PARTS):
        pre_pair(h, 0).wait_send()
        repeat(1, n_dp, lambda j: rs(h, j).wait_send())
        repeat(1, n_dp, lambda j: ag(h, j, d).wait_send())


def on_device(tokens, panel, cotangent):
    n_tok, depth_all = tokens.shape
    depth, cols = panel.shape
    n_tensor = lax.axis_size("tensor")
    n_dp = lax.axis_size("dp")
    n_z = n_tensor // 2
    scale = 1.0 / math.sqrt(n_tok * n_tensor * n_dp)
    chunk_rows = max(16, depth // n_dp)
    across = n_dp // (depth // chunk_rows)
    part = (PARTS, n_dp, chunk_rows, cols // PARTS // across)
    dma = pltpu.SemaphoreType.DMA
    vmem = pl.BlockSpec(memory_space=pltpu.VMEM)
    flops = 4 * n_tok * depth_all * cols
    hidden, grad = pl.pallas_call(
        functools.partial(kernel, n_dp, n_tensor, scale),
        out_shape=(
            jax.ShapeDtypeStruct((n_tok, cols // 2), jnp.float32),
            jax.ShapeDtypeStruct((depth, cols), jnp.bfloat16),
        ),
        in_specs=[vmem] * 3,
        out_specs=(vmem, vmem),
        scratch_shapes=[
            pltpu.VMEM((n_tensor, depth, cols), jnp.bfloat16),
            pltpu.VMEM((n_tensor, n_tok, depth), jnp.bfloat16),
            pltpu.VMEM((depth, n_tensor * n_tok), jnp.bfloat16),
            pltpu.VMEM((PARTS, n_tensor * n_tok, cols // PARTS), jnp.bfloat16),
            pltpu.VMEM((n_tok, cols), jnp.float32),
            pltpu.VMEM(part, jnp.bfloat16),
            pltpu.VMEM(part, jnp.bfloat16),
        ]
        + [dma((n_z,))] * 12
        + [dma((n_z, 2))] * 2
        + [dma((PARTS, n_z))] * 4
        + [dma((PARTS, n_dp))] * 4,
        compiler_params=pltpu.CompilerParams(
            collective_id=0, has_side_effects=True, vmem_limit_bytes=48 * 1024 * 1024
        ),
        cost_estimate=pl.CostEstimate(
            flops=flops, bytes_accessed=4 * depth * cols, transcendentals=n_tok * cols // 2
        ),
    )(tokens, panel, cotangent)
    return hidden, grad.astype(jnp.float32)


def solution(mesh):
    placed = (P(("dp", "tensor"), None), P("tensor", None), P(("dp", "tensor"), None))
    return jax.shard_map(
        on_device,
        mesh=mesh,
        in_specs=placed,
        out_specs=(P(("dp", "tensor"), None), P("tensor", None)),
        check_vma=False,
    )
```

time: 276 us -> 106 us (0.38)
  waiting for transfers between devices: 171 us -> 0 us
  Pallas kernels: 0 us -> 99.5 us
  blocking collectives: 75.2 us -> 0 us
  between operations: 14.1 us -> 0.65 us
  matrix products: 10.2 us -> 0 us
    pallas_call x0 -> x1, Pallas kernels: none -> 99.5 us  [on_device(): pl.pallas_call(functools.partial(kernel, n_dp, n_tensor, scale), out_shap...]
    reduce_scatter x1 -> x0, waiting for transfers between devices: 88.5 us -> none  [on_device(): lax.psum_scatter(grad_rows(tokens, pre_grad, scale).astype(jnp.bfloat16),...]
    all_gather x1 -> x0, waiting for transfers between devices: 82 us -> none  [on_device(): lax.all_gather(panel, 'tensor', axis=0, tiled=True)]
    psum x1 -> x0, blocking collectives: 75.2 us -> none  [on_device(): grad_panel = lax.psum(owned, 'dp')]
    dot_general x2 -> x0, matrix products: 10.2 us -> none  [the longest x1 5.6 us: grad_rows(): lax.dot_general(token_block, grad_block, (((0,), (0,)), ((), ())), prefer...]
  transfers between devices with their start and end apart: 2 -> 0, of which waited for: 2 -> 0; matrix products, arithmetic and copies ran while one was open for 0% -> 0% of each run, Pallas kernels for 0% -> 0%
where the time goes in v1:
time: 106 us
  Pallas kernels  99.5 us (94%)
  local copies, waits for them, and re-layouts  4.05 us (4%)
  other arithmetic  1.57 us (1%)
    pallas_call x1, Pallas kernels, on_device(): pl.pallas_call(functools.partial(kernel, n_dp, n_tensor, scale), out_shap...  99.5 us
    unnamed x7, local copies, waits for them, and re-layouts  4.05 us

profile of v1, /device:TPU:24, one launch (start us, length us, event | category | flops | bytes accessed | tf_op | source)
XLA Modules:
  0.0 105.8 jit_solution(9045165506036237836)
XLA Ops:
  0.6 0.0 copy-start
  0.6 1.2 %copy-done = bf16[128,4096]{1,0:T(8,128)(2,1)S(1)} copy-done((bf16[128,4096]{1,0:T(8,128)(2,1)S(1)}, bf16[128,4096]{1,0:T(8,128)(2,1)}, u32[]{:S(2)}) %copy-start) | copy-done | bytes 1048600
  1.9 0.0 copy-start.1
  1.9 1.2 %copy-done.1 = bf16[512,1024]{1,0:T(8,128)(2,1)S(1)} copy-done((bf16[512,1024]{1,0:T(8,128)(2,1)S(1)}, bf16[512,1024]{1,0:T(8,128)(2,1)}, u32[]{:S(2)}) %copy-start.1) | copy-done | bytes 1048600
  3.1 0.0 copy-start.2
  3.1 0.9 copy-done.2
  4.0 99.5 %shard_map.50 = (f32[128,512]{1,0:T(8,128)S(1)}, bf16[512,1024]{1,0:T(8,128)(2,1)S(1)}) custom-call(bf16[128,4096]{1,0:T(8,128)(2,1)S(1)} %copy-done, bf16[512,1024]{1,0:T(8,128)(2,1)S(1)} %copy-done.1, bf16[128,512]{1,0:T(8,128)(2,1)S(1)} %copy-done.2), custom_call_target="tpu_custom_call" | custom-call | flops 2147483648 | bytes 2097152 | tf_op jit(solution)/shard_map/pallas_call | solution.py:304
  103.5 1.6 %convert_element_type.3 = f32[512,1024]{1,0:T(8,128)} convert(bf16[512,1024]{1,0:T(8,128)(2,1)S(1)} %get-tuple-element.5) | non-fusion elementwise | flops 524288 | bytes 3145728 | tf_op jit(solution)/shard_map/convert_element_type | solution.py:332
  105.1 0.7 copy.6
Async XLA Ops:
  0.6 1.2 %copy-start = (bf16[128,4096]{1,0:T(8,128)(2,1)S(1)}, bf16[128,4096]{1,0:T(8,128)(2,1)}, u32[]{:S(2)}) copy-start(bf16[128,4096]{1,0:T(8,128)(2,1)} %tokens.1) | copy-start | bytes 3145732
  1.9 1.2 %copy-start.1 = (bf16[512,1024]{1,0:T(8,128)(2,1)S(1)}, bf16[512,1024]{1,0:T(8,128)(2,1)}, u32[]{:S(2)}) copy-start(bf16[512,1024]{1,0:T(8,128)(2,1)} %panel.1) | copy-start | bytes 3145732
  3.1 0.9 copy-start.2

commit v2 on v0

v2 whole, which is shorter than its diff:
```python
import functools
import math

import jax
import jax.numpy as jnp
from jax import lax
from jax.experimental import pallas as pl
from jax.experimental.pallas import tpu as pltpu
from jax.sharding import PartitionSpec as P

MESH = pl.DeviceIdType.MESH
LANES = 128


def repeat(low, high, body):
    if high - low <= 4:
        for i in range(low, high):
            body(i)
    else:
        lax.fori_loop(low, high, lambda i, carry: (body(i), carry)[1], 0)


def factor(n):
    return max(f for f in range(1, math.isqrt(n) + 1) if n % f == 0)


def kernel(
    n_dp, n_tensor, parts, scale,
    tokens, panel, cotangent,
    hidden, grad,
    tok_v, ct_v, hid_v, full, tok_all, tok_t, pre_all, acc, out_part, in_part, sum_v,
    in_sem, f1_s, f1_r, row_s, row_r, col_s, col_r, d0_s, d0_r, d1_s, d1_r, sib_s, sib_r,
    pair_s, pair_r, pre_s, pre_r, own_s, preo_s, tok_s, tok_r, rs_s, rs_r, ag_s, ag_r,
):
    n_tok, _ = tokens.shape
    depth, cols = panel.shape
    units = cols // 2
    width = cols // parts
    n_z = n_tensor // 2
    n_b = factor(n_dp)
    n_a = n_dp // n_b
    d, t = lax.axis_index("dp"), lax.axis_index("tensor")
    a, b = d // n_b, d % n_b
    z, c = t // 2, t % 2
    pair = z * 2 + 1 - c

    chunk_rows = max(16, depth // n_dp)
    down = depth // chunk_rows
    across = n_dp // down

    def chunk(i, span, half=None):
        wide = span // across
        row = pl.multiple_of((i // across) * chunk_rows, chunk_rows)
        start = (i % across) * wide
        if half is not None:
            wide = wide // 2
            start = start + half * wide
        return pl.ds(row, chunk_rows), pl.ds(pl.multiple_of(start, wide), wide)

    def send(src, dst, s, r, dp, tensor):
        return pltpu.make_async_remote_copy(
            src_ref=src, dst_ref=dst, send_sem=s, recv_sem=r,
            device_id=(dp, tensor), device_id_type=MESH,
        )

    def at_z(place, core):
        return place * 2 + core

    def arrival(n):
        short = jnp.minimum(z, n_z - 1 - z)
        both = n < 2 * short
        m = jnp.where(both, n // 2 + 1, n - short + 1)
        side = jnp.where(both, 2 * (n % 2) - 1, jnp.where(z > n_z - 1 - z, -1, 1))
        return z + side * m, z - side

    def inside(place):
        return (place >= 0) & (place < n_z)

    def f1_own(way):
        where = chunk(d, cols)
        to = at_z(z + 2 * way - 1, c)
        return send(panel.at[where], full.at[(t,) + where], own_s.at[way], f1_r.at[z], d, to)

    def f1(src, to):
        ref = full.at[(at_z(src, c),) + chunk(d, cols)]
        return send(ref, ref, f1_s.at[src], f1_r.at[src], d, at_z(to, c))

    def piece(src, i, s, r, to, half=None):
        ref = full.at[(at_z(src, c),) + chunk(i, cols, half)]
        return send(ref, ref, s.at[src], r.at[src], to, t)

    def a_peer(i):
        return ((a + i + n_a) % n_a) * n_b + b

    def b_peer(j):
        return a * n_b + (b + j + n_b) % n_b

    def ab_peer(i, j):
        return ((a + i + n_a) % n_a) * n_b + (b + j + n_b) % n_b

    def sib_own():
        return send(panel, full.at[t], sib_s.at[z], sib_r.at[z], d, pair)

    def sib(src, core):
        ref = full.at[at_z(src, core)]
        return send(ref, ref, sib_s.at[src], sib_r.at[src], d, pair)

    def far(k, core):
        return at_z((z + k + n_z) % n_z, core)

    def columns_of(i):
        return pl.ds(pl.multiple_of(i * depth, depth), depth)

    def rows_of(i):
        return pl.ds(pl.multiple_of(i * n_tok, n_tok), n_tok)

    def tok(k, other):
        to = far(k, (1 - c) if other else c)
        return send(
            tok_v.at[:, columns_of(to)], tok_all.at[t], tok_s.at[k, other], tok_r.at[k, other], d, to
        )

    def pre_own(p, way):
        ref = pre_all.at[p, rows_of(t)]
        to = at_z(z + 2 * way - 1, c)
        return send(ref, ref, preo_s.at[p, way], pre_r.at[p, z], d, to)

    def pre(p, src, to):
        ref = pre_all.at[p, rows_of(at_z(src, c))]
        return send(ref, ref, pre_s.at[p, src], pre_r.at[p, src], d, at_z(to, c))

    def pre_pair(p, src, core):
        ref = pre_all.at[p, rows_of(at_z(src, core))]
        return send(ref, ref, pair_s.at[p, src], pair_r.at[p, src], d, pair)

    def rs(p, j):
        to = (d + j) % n_dp
        return send(out_part.at[p, to], in_part.at[p, j], rs_s.at[p, j], rs_r.at[p, j], to, t)

    def place(p, i):
        row, col = chunk(i, width)
        return row, pl.ds(pl.multiple_of(p * width + col.start, col.size), col.size)

    def ag(p, j, i):
        return send(
            sum_v.at[p], grad.at[place(p, i)], ag_s.at[p, j], ag_r.at[p, j], (d + j) % n_dp, t
        )

    def both_ways(copy, act):
        pl.when(z > 0)(lambda: act(copy(0)))
        pl.when(z < n_z - 1)(lambda: act(copy(1)))

    def start(copy):
        copy.start()

    def gone(copy):
        copy.wait_send()

    tokens_in = pltpu.make_async_copy(tokens, tok_v, in_sem.at[0])
    panel_in = pltpu.make_async_copy(panel, full.at[t], in_sem.at[1])
    ct_in = pltpu.make_async_copy(cotangent, ct_v, in_sem.at[2])
    tokens_in.start()
    panel_in.start()
    ct_in.start()

    barrier = pltpu.get_barrier_semaphore()

    def greet_tensor(k):
        pl.semaphore_signal(barrier, inc=1, device_id=(d, (t + k) % n_tensor), device_id_type=MESH)

    def greet_dp(k):
        pl.semaphore_signal(barrier, inc=1, device_id=((d + k) % n_dp, t), device_id_type=MESH)

    repeat(1, n_tensor, greet_tensor)
    repeat(1, n_dp, greet_dp)
    pl.semaphore_wait(barrier, n_tensor + n_dp - 2)

    both_ways(f1_own, start)
    sib_own().start()
    tokens_in.wait()
    panel_in.wait()
    ct_in.wait()
    tok(0, 1).start()

    def multiply(own):
        return jnp.dot(tok_v[:, columns_of(own)], full[own], preferred_element_type=jnp.float32)

    acc[...] = multiply(t)

    def spread(n):
        src, to = arrival(n)
        f1(src, to).wait_recv()
        pl.when(inside(to))(lambda: f1(src, to).start())
        repeat(1, n_b, lambda j: piece(src, d, row_s, row_r, b_peer(j)).start())
        repeat(1, n_a, lambda i: piece(src, d, col_s, col_r, a_peer(i)).start())
        tok(n + 1, 0).start()
        tok(n + 1, 1).start()

    def relay(n):
        src, _ = arrival(n)
        repeat(1, n_b, lambda j: piece(src, b_peer(-j), row_s, row_r, d).wait_recv())

        def pass_a(j):
            repeat(1, n_a, lambda i: piece(src, b_peer(-j), d0_s, d0_r, a_peer(i), 0).start())

        repeat(1, n_b, pass_a)
        repeat(1, n_a, lambda i: piece(src, a_peer(-i), col_s, col_r, d).wait_recv())

        def pass_b(i):
            repeat(1, n_b, lambda j: piece(src, a_peer(-i), d1_s, d1_r, b_peer(j), 1).start())

        repeat(1, n_a, pass_b)

    def finish(n):
        src, _ = arrival(n)

        def corner(i):
            def corner_b(j):
                piece(src, ab_peer(-i, -j), d0_s, d0_r, d, 0).wait_recv()
                piece(src, ab_peer(-i, -j), d1_s, d1_r, d, 1).wait_recv()
            repeat(1, n_b, corner_b)
        repeat(1, n_a, corner)
        sib(src, c).start()
        acc[...] += multiply(at_z(src, c))

    def other(src):
        sib(src, 1 - c).wait_recv()
        acc[...] += multiply(at_z(src, 1 - c))

    def when(n, body):
        if isinstance(n, int):
            if 0 <= n < n_z - 1:
                body(n)
        else:
            pl.when((n >= 0) & (n < n_z - 1))(lambda: body(n))

    def stage(n):
        when(n, spread)
        when(n - 1, relay)
        when(n - 2, finish)
        when(n - 3, lambda m: other(arrival(m)[0]))

    stage(0)
    other(z)
    repeat(1, n_z + 2, stage)

    gate = acc[:, :units]
    up = acc[:, units:]
    s = jax.nn.sigmoid(gate)
    act = gate * s
    ct = ct_v[...].astype(jnp.float32)
    gate_grad = (ct * up * s * (1.0 + gate * (1.0 - s))).astype(jnp.bfloat16)
    up_grad = (ct * act).astype(jnp.bfloat16)
    for p in range(parts):
        term = gate_grad if p < parts // 2 else up_grad
        first = (p % (parts // 2)) * width
        pre_all[p, rows_of(t), :] = term[:, first:first + width]
        if p < 2:
            both_ways(lambda way: pre_own(p, way), start)
            pre_pair(p, z, c).start()
    hid_v[...] = act * up
    hidden_out = pltpu.make_async_copy(hid_v, hidden, in_sem.at[3])
    hidden_out.start()

    tok_t[:, rows_of(t)] = tok_v[:, columns_of(t)].T

    def take(own, k, index):
        dst = tok_all.at[own]
        send(dst, dst, tok_s.at[k, index], tok_r.at[k, index], d, pair).wait_recv()
        tok_t[:, rows_of(own)] = dst[...].T

    take(pair, 0, 1)

    def take_both(k):
        take(far(-k, c), k, 0)
        take(far(-k, 1 - c), k, 1)

    def arrive(p, n):
        src, to = arrival(n)
        pre(p, src, to).wait_recv()
        pl.when(inside(to))(lambda: pre(p, src, to).start())
        pre_pair(p, src, c).start()

    def product(p):
        repeat(0, n_z, lambda src: pre_pair(p, src, 1 - c).wait_recv())

        def rows(i):
            row, col = chunk(i, width)
            term = jnp.dot(tok_t[row, :], pre_all[p, :, col], preferred_element_type=jnp.float32)
            out_part[p, i] = (term * scale).astype(jnp.bfloat16)

        repeat(0, n_dp, rows)
        repeat(1, n_dp, lambda j: rs(p, j).start())

    def own_sum(p):
        return pltpu.make_async_copy(sum_v.at[p], grad.at[place(p, d)], in_sem.at[4 + p])

    def reduce(p):
        repeat(1, n_dp, lambda j: rs(p, j).wait_recv())
        total = out_part[p, d].astype(jnp.float32)
        for j in range(1, n_dp):
            total = total + in_part[p, j].astype(jnp.float32)
        sum_v[p] = total.astype(jnp.bfloat16)
        repeat(1, n_dp, lambda j: ag(p, j, d).start())
        own_sum(p).start()

    last = n_z - 2
    for p in range(parts):
        if p == 0:
            repeat(0, last, lambda n: arrive(0, n))
            repeat(1, n_z, take_both)
        if p + 1 < parts:
            arrive(p + 1, 0)
        arrive(p, last)
        if p + 2 < parts:
            both_ways(lambda way: pre_own(p + 2, way), start)
            pre_pair(p + 2, z, c).start()
        if p + 1 < parts:
            repeat(1, last, lambda n: arrive(p + 1, n))
        product(p)
        if p > 0:
            reduce(p - 1)
    reduce(parts - 1)
    for p in range(parts):
        repeat(1, n_dp, lambda j: ag(p, j, (d - j + n_dp) % n_dp).wait_recv())
        own_sum(p).wait()

    hidden_out.wait()
    both_ways(f1_own, gone)
    sib_own().wait_send()
    tok(0, 1).wait_send()
    for p in range(parts):
        both_ways(lambda way: pre_own(p, way), gone)
        pre_pair(p, z, c).wait_send()
        repeat(1, n_dp, lambda j: rs(p, j).wait_send())
        repeat(1, n_dp, lambda j: ag(p, j, d).wait_send())

    def sent(n):
        src, to = arrival(n)
        pl.when(inside(to))(lambda: f1(src, to).wait_send())
        repeat(1, n_b, lambda j: piece(src, d, row_s, row_r, b_peer(j)).wait_send())
        repeat(1, n_a, lambda i: piece(src, d, col_s, col_r, a_peer(i)).wait_send())

        def corner(i):
            def corner_b(j):
                piece(src, b_peer(-j), d0_s, d0_r, a_peer(i), 0).wait_send()
                piece(src, a_peer(-i), d1_s, d1_r, b_peer(j), 1).wait_send()
            repeat(1, n_b, corner_b)
        repeat(1, n_a, corner)
        sib(src, c).wait_send()
        tok(n + 1, 0).wait_send()
        tok(n + 1, 1).wait_send()
        for p in range(parts):
            pl.when(inside(to))(lambda: pre(p, src, to).wait_send())
            pre_pair(p, src, c).wait_send()

    repeat(0, n_z - 1, sent)


def on_device(tokens, panel, cotangent):
    n_tok, depth_all = tokens.shape
    depth, cols = panel.shape
    n_tensor = lax.axis_size("tensor")
    n_dp = lax.axis_size("dp")
    n_z = n_tensor // 2
    scale = 1.0 / math.sqrt(n_tok * n_tensor * n_dp)
    chunk_rows = max(16, depth // n_dp)
    across = n_dp // (depth // chunk_rows)
    parts = max(p for p in (2, 4) if (cols // p // across) % LANES == 0)
    part = (parts, n_dp, chunk_rows, cols // parts // across)
    dma = pltpu.SemaphoreType.DMA
    anywhere = pl.BlockSpec(memory_space=pl.ANY)
    bf16, f32 = jnp.bfloat16, jnp.float32
    hidden, grad = pl.pallas_call(
        functools.partial(kernel, n_dp, n_tensor, parts, scale),
        out_shape=(
            jax.ShapeDtypeStruct((n_tok, cols // 2), f32),
            jax.ShapeDtypeStruct((depth, cols), bf16),
        ),
        in_specs=[anywhere] * 3,
        out_specs=(anywhere, anywhere),
        scratch_shapes=[
            pltpu.VMEM((n_tok, depth_all), bf16),
            pltpu.VMEM((n_tok, cols // 2), bf16),
            pltpu.VMEM((n_tok, cols // 2), f32),
            pltpu.VMEM((n_tensor, depth, cols), bf16),
            pltpu.VMEM((n_tensor, n_tok, depth), bf16),
            pltpu.VMEM((depth, n_tensor * n_tok), bf16),
            pltpu.VMEM((parts, n_tensor * n_tok, cols // parts), bf16),
            pltpu.VMEM((n_tok, cols), f32),
            pltpu.VMEM(part, bf16),
            pltpu.VMEM(part, bf16),
            pltpu.VMEM((parts,) + part[2:], bf16),
        ]
        + [dma((4 + parts,))]
        + [dma((n_z,))] * 12
        + [dma((parts, n_z))] * 4
        + [dma((2,)), dma((parts, 2))]
        + [dma((n_z, 2))] * 2
        + [dma((parts, n_dp))] * 4,
        compiler_params=pltpu.CompilerParams(
            collective_id=0, has_side_effects=True, vmem_limit_bytes=60 * 1024 * 1024
        ),
        cost_estimate=pl.CostEstimate(
            flops=4 * n_tok * depth_all * cols,
            bytes_accessed=4 * depth * cols,
            transcendentals=n_tok * cols // 2,
        ),
    )(tokens, panel, cotangent)
    return hidden, grad.astype(jnp.float32)


def solution(mesh):
    placed = (P(("dp", "tensor"), None), P("tensor", None), P(("dp", "tensor"), None))
    return jax.shard_map(
        on_device,
        mesh=mesh,
        in_specs=placed,
        out_specs=(P(("dp", "tensor"), None), P("tensor", None)),
        check_vma=False,
    )
```

time: 276 us -> 106 us (0.38)
  the two profiles are of different devices: /device:TPU:24 before, /device:TPU:0 now
where the time goes in v2:
time: 106 us
  Pallas kernels  101 us (95%)
  other arithmetic  2.83 us (3%)
    pallas_call x1, Pallas kernels, on_device(): pl.pallas_call(functools.partial(kernel, n_dp, n_tensor, parts, scale), o...  101 us
    convert_element_type x1, other arithmetic, on_device(): return (hidden, grad.astype(jnp.float32))  2.83 us

profile of v2, /device:TPU:0, one launch (start us, length us, event | category | flops | bytes accessed | tf_op | source)
XLA Modules:
  0.0 105.6 jit_solution(16074823388250390584)
XLA Ops:
  0.6 101.4 %shard_map.50 = (f32[128,512]{1,0:T(8,128)}, bf16[512,1024]{1,0:T(8,128)(2,1)}) custom-call(bf16[128,4096]{1,0:T(8,128)(2,1)} %tokens.1, bf16[512,1024]{1,0:T(8,128)(2,1)} %panel.1, bf16[128,512]{1,0:T(8,128)(2,1)} %cotangent.1), custom_call_target="tpu_custom_call" | custom-call | flops 2147483648 | bytes 2097152 | tf_op jit(solution)/shard_map/pallas_call | solution.py:374
  102.0 0.0 copy-start
  102.0 2.8 %convert_element_type.3 = f32[512,1024]{1,0:T(8,128)} convert(bf16[512,1024]{1,0:T(8,128)(2,1)} %get-tuple-element.5) | non-fusion elementwise | flops 524288 | bytes 3145728 | tf_op jit(solution)/shard_map/convert_element_type | solution.py:410
  104.9 0.0 copy-done
  104.9 0.7 copy.6
Async XLA Ops:
  102.0 2.8 %copy-start = (f32[128,512]{1,0:T(8,128)S(1)}, f32[128,512]{1,0:T(8,128)}, u32[]{:S(2)}) copy-start(f32[128,512]{1,0:T(8,128)} %get-tuple-element.8) | copy-start | bytes 786436

commit v3 on v2

--- a/solution.py
+++ b/solution.py
@@ -9,7 +9,6 @@
 from jax.sharding import PartitionSpec as P
 
 MESH = pl.DeviceIdType.MESH
-LANES = 128
 
 
 def repeat(low, high, body):
@@ -28,7 +27,7 @@
     n_dp, n_tensor, parts, scale,
     tokens, panel, cotangent,
     hidden, grad,
-    tok_v, ct_v, hid_v, full, tok_all, tok_t, pre_all, acc, out_part, in_part, sum_v,
+    tok_v, ct_v, hid_v, full, tok_all, tok_t, pre_all, acc, out_part, in_part,
     in_sem, f1_s, f1_r, row_s, row_r, col_s, col_r, d0_s, d0_r, d1_s, d1_r, sib_s, sib_r,
     pair_s, pair_r, pre_s, pre_r, own_s, preo_s, tok_s, tok_r, rs_s, rs_r, ag_s, ag_r,
 ):
@@ -142,9 +141,8 @@
         return row, pl.ds(pl.multiple_of(p * width + col.start, col.size), col.size)
 
     def ag(p, j, i):
-        return send(
-            sum_v.at[p], grad.at[place(p, i)], ag_s.at[p, j], ag_r.at[p, j], (d + j) % n_dp, t
-        )
+        ref = grad.at[place(p, i)]
+        return send(ref, ref, ag_s.at[p, j], ag_r.at[p, j], (d + j) % n_dp, t)
 
     def both_ways(copy, act):
         pl.when(z > 0)(lambda: act(copy(0)))
@@ -193,8 +191,10 @@
         pl.when(inside(to))(lambda: f1(src, to).start())
         repeat(1, n_b, lambda j: piece(src, d, row_s, row_r, b_peer(j)).start())
         repeat(1, n_a, lambda i: piece(src, d, col_s, col_r, a_peer(i)).start())
-        tok(n + 1, 0).start()
-        tok(n + 1, 1).start()
+
+    def exchange(k):
+        tok(k, 0).start()
+        tok(k, 1).start()
 
     def relay(n):
         src, _ = arrival(n)
@@ -237,6 +237,11 @@
     def stage(n):
         when(n, spread)
         when(n - 1, relay)
+        if isinstance(n, int):
+            if n == n_z - 1:
+                repeat(1, n_z, exchange)
+        else:
+            pl.when(n == n_z - 1)(lambda: repeat(1, n_z, exchange))
         when(n - 2, finish)
         when(n - 3, lambda m: other(arrival(m)[0]))
 
@@ -292,17 +297,13 @@
         repeat(0, n_dp, rows)
         repeat(1, n_dp, lambda j: rs(p, j).start())
 
-    def own_sum(p):
-        return pltpu.make_async_copy(sum_v.at[p], grad.at[place(p, d)], in_sem.at[4 + p])
-
     def reduce(p):
         repeat(1, n_dp, lambda j: rs(p, j).wait_recv())
         total = out_part[p, d].astype(jnp.float32)
         for j in range(1, n_dp):
             total = total + in_part[p, j].astype(jnp.float32)
-        sum_v[p] = total.astype(jnp.bfloat16)
+        grad[place(p, d)] = total.astype(jnp.bfloat16)
         repeat(1, n_dp, lambda j: ag(p, j, d).start())
-        own_sum(p).start()
 
     last = n_z - 2
     for p in range(parts):
@@ -323,7 +324,6 @@
     reduce(parts - 1)
     for p in range(parts):
         repeat(1, n_dp, lambda j: ag(p, j, (d - j + n_dp) % n_dp).wait_recv())
-        own_sum(p).wait()
 
     hidden_out.wait()
     both_ways(f1_own, gone)
@@ -366,7 +366,7 @@
     scale = 1.0 / math.sqrt(n_tok * n_tensor * n_dp)
     chunk_rows = max(16, depth // n_dp)
     across = n_dp // (depth // chunk_rows)
-    parts = max(p for p in (2, 4) if (cols // p // across) % LANES == 0)
+    parts = 2
     part = (parts, n_dp, chunk_rows, cols // parts // across)
     dma = pltpu.SemaphoreType.DMA
     anywhere = pl.BlockSpec(memory_space=pl.ANY)
@@ -378,7 +378,7 @@
             jax.ShapeDtypeStruct((depth, cols), bf16),
         ),
         in_specs=[anywhere] * 3,
-        out_specs=(anywhere, anywhere),
+        out_specs=(anywhere, pl.BlockSpec(memory_space=pltpu.VMEM)),
         scratch_shapes=[
             pltpu.VMEM((n_tok, depth_all), bf16),
             pltpu.VMEM((n_tok, cols // 2), bf16),
@@ -390,9 +390,8 @@
             pltpu.VMEM((n_tok, cols), f32),
             pltpu.VMEM(part, bf16),
             pltpu.VMEM(part, bf16),
-            pltpu.VMEM((parts,) + part[2:], bf16),
         ]
-        + [dma((4 + parts,))]
+        + [dma((4,))]
         + [dma((n_z,))] * 12
         + [dma((parts, n_z))] * 4
         + [dma((2,)), dma((parts, 2))]

time: 106 us -> 106 us (level)
  no operation moved by 1% of the time
where the time goes in v3:
time: 106 us
  Pallas kernels  102 us (96%)
  other arithmetic  2.83 us (3%)
    pallas_call x1, Pallas kernels, on_device(): pl.pallas_call(functools.partial(kernel, n_dp, n_tensor, parts, scale), o...  102 us
    convert_element_type x1, other arithmetic, on_device(): return (hidden, grad.astype(jnp.float32))  2.83 us

profile of v3, /device:TPU:0, one launch (start us, length us, event | category | flops | bytes accessed | tf_op | source)
XLA Modules:
  0.0 105.8 jit_solution(8612863705278442912)
XLA Ops:
  0.6 101.6 %shard_map.50 = (f32[128,512]{1,0:T(8,128)}, bf16[512,1024]{1,0:T(8,128)(2,1)}) custom-call(bf16[128,4096]{1,0:T(8,128)(2,1)} %tokens.1, bf16[512,1024]{1,0:T(8,128)(2,1)} %panel.1, bf16[128,512]{1,0:T(8,128)(2,1)} %cotangent.1), custom_call_target="tpu_custom_call" | custom-call | flops 2147483648 | bytes 2097152 | tf_op jit(solution)/shard_map/pallas_call | solution.py:374
  102.3 0.0 copy-start
  102.3 2.8 %convert_element_type.3 = f32[512,1024]{1,0:T(8,128)} convert(bf16[512,1024]{1,0:T(8,128)(2,1)} %get-tuple-element.5) | non-fusion elementwise | flops 524288 | bytes 3145728 | tf_op jit(solution)/shard_map/convert_element_type | solution.py:409
  105.1 0.0 copy-done
  105.1 0.7 copy.6
Async XLA Ops:
  102.3 2.8 %copy-start = (f32[128,512]{1,0:T(8,128)S(1)}, f32[128,512]{1,0:T(8,128)}, u32[]{:S(2)}) copy-start(f32[128,512]{1,0:T(8,128)} %get-tuple-element.8) | copy-start | bytes 786436

commit v4 on v0

v4 whole, which is shorter than its diff:
```python
import functools
import math

import jax
import jax.numpy as jnp
from jax import lax
from jax.experimental import pallas as pl
from jax.experimental.pallas import tpu as pltpu
from jax.sharding import PartitionSpec as P

MESH = pl.DeviceIdType.MESH
PARTS = 2
LANES = 128


def repeat(low, high, body):
    if high - low <= 4:
        for i in range(low, high):
            body(i)
    else:
        lax.fori_loop(low, high, lambda i, carry: (body(i), carry)[1], 0)


def team_size(n_dp, depth):
    return max(s for s in range(1, n_dp + 1) if n_dp % s == 0 and depth % (s * LANES) == 0)


def kernel(
    n_dp, n_tensor, n_s, scale,
    tokens, panel, cotangent,
    hidden, grad,
    tok_v, ct_v, hid_v, stage, tok_x, tok_t, pan, mate_out, mate_in, sum_out, sum_in, own_part,
    proj, pre_all, row_own, row_out, row_in, team_in,
    in_sem, own_s, pan_s, pan_r, tok_s, tok_r, mate_s, mate_r, sum_s, sum_r,
    pre_s, pre_r, pair_s, pair_r, row_s, row_r, team_s, team_r, ag_s, ag_r,
):
    n_tok, _ = tokens.shape
    depth, cols = panel.shape
    width = cols // PARTS
    n_z = n_tensor // 2
    n_g = n_dp // n_s
    r = depth // n_s
    d, t = lax.axis_index("dp"), lax.axis_index("tensor")
    g, s = d // n_s, d % n_s
    z, c = t // 2, t % 2
    pair = z * 2 + 1 - c

    def send(src, dst, s_sem, r_sem, dp, tensor):
        return pltpu.make_async_remote_copy(
            src_ref=src, dst_ref=dst, send_sem=s_sem, recv_sem=r_sem,
            device_id=(dp, tensor), device_id_type=MESH,
        )

    def arrival(n):
        short = jnp.minimum(z, n_z - 1 - z)
        both = n < 2 * short
        m = jnp.where(both, n // 2 + 1, n - short + 1)
        side = jnp.where(both, 2 * (n % 2) - 1, jnp.where(z > n_z - 1 - z, -1, 1))
        return z + side * m, z - side

    def inside(place):
        return (place >= 0) & (place < n_z)

    def slots(i, size):
        return pl.ds(pl.multiple_of(i * size, size), size)

    def mate(j):
        return (s + j) % n_s

    def dp_of(i):
        return g * n_s + i

    def part(p):
        return pl.ds(p * width, width)

    def pan_own(way):
        to = (z + 2 * way - 1) * 2 + c
        return send(panel.at[slots(s, r)], pan.at[slots(z, r)], own_s.at[way], pan_r.at[z], d, to)

    def pan_on(src, to):
        ref = pan.at[slots(src, r)]
        return send(ref, ref, pan_s.at[src], pan_r.at[src], d, to * 2 + c)

    my_slot = c * n_s + s

    def tok(k):
        e = (my_slot + k) % (2 * n_s)
        return send(
            stage.at[e], tok_x.at[slots(my_slot, n_tok)], tok_s.at[k], tok_r.at[k],
            dp_of(e % n_s), z * 2 + e // n_s,
        )

    def halfway(p):
        return send(mate_out.at[p], mate_in.at[p], mate_s.at[p], mate_r.at[p], d, pair)

    def sums(p, j):
        to = mate(j)
        return send(
            sum_out.at[p, slots(to, n_tok)], sum_in.at[p, j], sum_s.at[p, j], sum_r.at[p, j], dp_of(to), t
        )

    def pre(p, j, owner):
        ref = pre_all.at[p, slots(c * n_s + owner, n_tok)]
        return send(ref, ref, pre_s.at[p, j], pre_r.at[p, j], dp_of(mate(j)), t)

    def pre_pair(p, j, core):
        ref = pre_all.at[p, slots(core * n_s + mate(-j + n_s), n_tok)]
        return send(ref, ref, pair_s.at[p, j], pair_r.at[p, j], d, pair)

    def rows_to(p, k):
        to = (z + k) % n_z
        return send(
            row_out.at[p, slots(to, r)], row_in.at[p, k], row_s.at[p, k], row_r.at[p, k], d, to * 2 + c
        )

    def team(p, k):
        return send(
            team_in.at[p, g], team_in.at[p, g], team_s.at[p, k], team_r.at[p, k],
            ((g + k) % n_g) * n_s + s, t,
        )

    def ag(p, j, owner):
        ref = grad.at[slots(owner, r), part(p)]
        return send(ref, ref, ag_s.at[p, j], ag_r.at[p, j], dp_of(mate(j)), t)

    def both_ways(copy, act):
        pl.when(z > 0)(lambda: act(copy(0)))
        pl.when(z < n_z - 1)(lambda: act(copy(1)))

    tokens_in = pltpu.make_async_copy(tokens, tok_v, in_sem.at[0])
    panel_in = pltpu.make_async_copy(panel.at[slots(s, r)], pan.at[slots(z, r)], in_sem.at[1])
    ct_in = pltpu.make_async_copy(cotangent, ct_v, in_sem.at[2])
    tokens_in.start()
    panel_in.start()
    ct_in.start()

    barrier = pltpu.get_barrier_semaphore()

    def greet(dp, tensor):
        pl.semaphore_signal(barrier, inc=1, device_id=(dp, tensor), device_id_type=MESH)

    def greet_plane(k):
        e = (my_slot + k) % (2 * n_s)
        greet(dp_of(e % n_s), z * 2 + e // n_s)

    repeat(1, n_z, lambda k: greet(d, ((z + k) % n_z) * 2 + c))
    repeat(1, 2 * n_s, greet_plane)
    repeat(1, n_g, lambda k: greet(((g + k) % n_g) * n_s + s, t))
    pl.semaphore_wait(barrier, n_z + 2 * n_s + n_g - 3)

    both_ways(pan_own, lambda copy: copy.start())
    tokens_in.wait()

    for e in range(2 * n_s):
        for i in range(n_z):
            first = (i * 2 + e // n_s) * depth + (e % n_s) * r
            stage[e, :, i * r:(i + 1) * r] = tok_v[:, first:first + r]
    repeat(1, 2 * n_s, lambda k: tok(k).start())
    tok_x[slots(my_slot, n_tok), :] = stage[my_slot]
    tok_t[:, slots(my_slot, n_tok)] = stage[my_slot].T

    def pass_on(n):
        src, to = arrival(n)
        pan_on(src, to).wait_recv()
        pl.when(inside(to))(lambda: pan_on(src, to).start())

    def take(k):
        e = (my_slot - k + 2 * n_s) % (2 * n_s)
        ref = tok_x.at[slots(e, n_tok)]
        send(ref, ref, tok_s.at[k], tok_r.at[k], d, pair).wait_recv()
        tok_t[:, slots(e, n_tok)] = ref[...].T

    if n_z > 1:
        pass_on(0)
    repeat(1, n_s, take)
    repeat(1, n_z - 2, pass_on)
    repeat(n_s, 2 * n_s, take)
    if n_z > 2:
        pass_on(n_z - 2)
    panel_in.wait()
    ct_in.wait()

    team_rows = n_s * n_tok
    for p in range(PARTS):
        mate_out[p] = jnp.dot(
            tok_x[slots(1 - c, team_rows), :], pan[:, part(p)], preferred_element_type=jnp.float32
        ).astype(jnp.bfloat16)
        halfway(p).start()
    for p in range(PARTS):
        own_part[...] = jnp.dot(
            tok_x[slots(c, team_rows), :], pan[:, part(p)], preferred_element_type=jnp.float32
        )
        halfway(p).wait_recv()
        own_part[...] += mate_in[p].astype(jnp.float32)
        sum_out[p] = own_part[...].astype(jnp.bfloat16)
        repeat(1, n_s, lambda j: sums(p, j).start())
        proj[:, part(p)] = own_part[slots(s, n_tok), :]
    for p in range(PARTS):
        def add(j):
            sums(p, j).wait_recv()
            proj[:, part(p)] += sum_in[p, j].astype(jnp.float32)

        repeat(1, n_s, add)

    gate = proj[:, part(0)]
    up = proj[:, part(1)]
    sig = jax.nn.sigmoid(gate)
    act = gate * sig
    ct = ct_v[...].astype(jnp.float32)
    pre_all[0, slots(my_slot, n_tok), :] = (ct * up * sig * (1.0 + gate * (1.0 - sig))).astype(jnp.bfloat16)
    pre_all[1, slots(my_slot, n_tok), :] = (ct * act).astype(jnp.bfloat16)
    for p in range(PARTS):
        repeat(1, n_s, lambda j: pre(p, j, s).start())
        pre_pair(p, 0, c).start()
    hid_v[...] = act * up
    hidden_out = pltpu.make_async_copy(hid_v, hidden, in_sem.at[3])
    hidden_out.start()

    def finish(p):
        own_rows = row_own.at[p]

        def add(k):
            rows_to(p, k).wait_recv()
            own_rows[...] += row_in[p, k].astype(jnp.float32)

        repeat(1, n_z, add)
        if n_g > 1:
            team_in[p, g] = own_rows[...].astype(jnp.bfloat16)
            repeat(1, n_g, lambda k: team(p, k).start())

            def others(k):
                ref = team_in.at[p, (g - k + n_g) % n_g]
                send(ref, ref, team_s.at[p, k], team_r.at[p, k], d, pair).wait_recv()

            repeat(1, n_g, others)
            own_rows[...] = jnp.zeros((r, width), jnp.float32)

            def add_team(i):
                own_rows[...] += team_in[p, i].astype(jnp.float32)

            repeat(0, n_g, add_team)
        grad[slots(s, r), part(p)] = own_rows[...].astype(jnp.bfloat16)
        repeat(1, n_s, lambda j: ag(p, j, s).start())

    for p in range(PARTS):
        def arrive(j):
            pre(p, j, mate(-j + n_s)).wait_recv()
            pre_pair(p, j, c).start()

        repeat(1, n_s, arrive)
        repeat(0, n_s, lambda j: pre_pair(p, j, 1 - c).wait_recv())

        def product(k):
            to = (z + k) % n_z
            return scale * jnp.dot(
                tok_t[slots(to, r), :], pre_all[p], preferred_element_type=jnp.float32
            )

        def product_out(k):
            row_out[p, slots((z + k) % n_z, r), :] = product(k).astype(jnp.bfloat16)
            rows_to(p, k).start()

        repeat(1, n_z, product_out)
        row_own[p] = product(0)
    for p in range(PARTS):
        finish(p)
    for p in range(PARTS):
        repeat(1, n_s, lambda j: ag(p, j, mate(-j + n_s)).wait_recv())

    hidden_out.wait()
    both_ways(pan_own, lambda copy: copy.wait_send())

    def passed_on(n):
        src, to = arrival(n)
        pl.when(inside(to))(lambda: pan_on(src, to).wait_send())

    repeat(0, n_z - 1, passed_on)
    repeat(1, 2 * n_s, lambda k: tok(k).wait_send())
    for p in range(PARTS):
        halfway(p).wait_send()
        repeat(1, n_z, lambda k: rows_to(p, k).wait_send())
        repeat(1, n_g, lambda k: team(p, k).wait_send())
        repeat(0, n_s, lambda j: pre_pair(p, j, c).wait_send())

        def sent(j):
            sums(p, j).wait_send()
            pre(p, j, s).wait_send()
            ag(p, j, s).wait_send()

        repeat(1, n_s, sent)


def on_device(tokens, panel, cotangent):
    n_tok, depth_all = tokens.shape
    depth, cols = panel.shape
    n_tensor = lax.axis_size("tensor")
    n_dp = lax.axis_size("dp")
    n_z = n_tensor // 2
    n_s = team_size(n_dp, depth)
    n_g = n_dp // n_s
    r = depth // n_s
    scale = 1.0 / math.sqrt(n_tok * n_tensor * n_dp)
    width = cols // PARTS
    team = n_s * n_tok
    dma = pltpu.SemaphoreType.DMA
    anywhere = pl.BlockSpec(memory_space=pl.ANY)
    bf16, f32 = jnp.bfloat16, jnp.float32
    hidden, grad = pl.pallas_call(
        functools.partial(kernel, n_dp, n_tensor, n_s, scale),
        out_shape=(
            jax.ShapeDtypeStruct((n_tok, cols // 2), f32),
            jax.ShapeDtypeStruct((depth, cols), bf16),
        ),
        in_specs=[anywhere] * 3,
        out_specs=(anywhere, pl.BlockSpec(memory_space=pltpu.VMEM)),
        scratch_shapes=[
            pltpu.VMEM((n_tok, depth_all), bf16),
            pltpu.VMEM((n_tok, cols // 2), bf16),
            pltpu.VMEM((n_tok, cols // 2), f32),
            pltpu.VMEM((2 * n_s, n_tok, n_z * r), bf16),
            pltpu.VMEM((2 * team, n_z * r), bf16),
            pltpu.VMEM((n_z * r, 2 * team), bf16),
            pltpu.VMEM((n_z * r, cols), bf16),
            pltpu.VMEM((PARTS, team, width), bf16),
            pltpu.VMEM((PARTS, team, width), bf16),
            pltpu.VMEM((PARTS, team, width), bf16),
            pltpu.VMEM((PARTS, n_s, n_tok, width), bf16),
            pltpu.VMEM((team, width), f32),
            pltpu.VMEM((n_tok, cols), f32),
            pltpu.VMEM((PARTS, 2 * team, width), bf16),
            pltpu.VMEM((PARTS, r, width), f32),
            pltpu.VMEM((PARTS, n_z * r, width), bf16),
            pltpu.VMEM((PARTS, n_z, r, width), bf16),
            pltpu.VMEM((PARTS, n_g, r, width), bf16),
        ]
        + [dma((4,)), dma((2,)), dma((n_z,)), dma((n_z,)), dma((2 * n_s,)), dma((2 * n_s,))]
        + [dma((PARTS,))] * 2
        + [dma((PARTS, n_s))] * 6
        + [dma((PARTS, n_z))] * 2
        + [dma((PARTS, n_g))] * 2
        + [dma((PARTS, n_s))] * 2,
        compiler_params=pltpu.CompilerParams(
            collective_id=0, has_side_effects=True, vmem_limit_bytes=60 * 1024 * 1024
        ),
        cost_estimate=pl.CostEstimate(
            flops=4 * n_tok * depth_all * cols,
            bytes_accessed=4 * depth * cols,
            transcendentals=n_tok * cols // 2,
        ),
    )(tokens, panel, cotangent)
    return hidden, grad.astype(jnp.float32)


def solution(mesh):
    placed = (P(("dp", "tensor"), None), P("tensor", None), P(("dp", "tensor"), None))
    return jax.shard_map(
        on_device,
        mesh=mesh,
        in_specs=placed,
        out_specs=(P(("dp", "tensor"), None), P("tensor", None)),
        check_vma=False,
    )
```

time: 276 us -> 84.2 us (0.31)
  waiting for transfers between devices: 171 us -> 0 us
  Pallas kernels: 0 us -> 79.8 us
  blocking collectives: 75.2 us -> 0 us
  between operations: 14.1 us -> 0.65 us
  matrix products: 10.2 us -> 0 us
    reduce_scatter x1 -> x0, waiting for transfers between devices: 88.5 us -> none  [on_device(): lax.psum_scatter(grad_rows(tokens, pre_grad, scale).astype(jnp.bfloat16),...]
    all_gather x1 -> x0, waiting for transfers between devices: 82 us -> none  [on_device(): lax.all_gather(panel, 'tensor', axis=0, tiled=True)]
    pallas_call x0 -> x1, Pallas kernels: none -> 79.8 us  [on_device(): pl.pallas_call(functools.partial(kernel, n_dp, n_tensor, n_s, scale), out...]
    psum x1 -> x0, blocking collectives: 75.2 us -> none  [on_device(): grad_panel = lax.psum(owned, 'dp')]
    dot_general x2 -> x0, matrix products: 10.2 us -> none  [the longest x1 5.6 us: grad_rows(): lax.dot_general(token_block, grad_block, (((0,), (0,)), ((), ())), prefer...]
    convert_element_type x0 -> x1, other arithmetic: none -> 2.83 us  [on_device(): return (hidden, grad.astype(jnp.float32))]
  transfers between devices with their start and end apart: 2 -> 0, of which waited for: 2 -> 0; matrix products, arithmetic and copies ran while one was open for 0% -> 0% of each run, Pallas kernels for 0% -> 0%
where the time goes in v4:
time: 84.2 us; the launch traced here: 84 us
  Pallas kernels  79.8 us (95%)
  other arithmetic  2.83 us (3%)
    pallas_call x1, Pallas kernels, on_device(): pl.pallas_call(functools.partial(kernel, n_dp, n_tensor, n_s, scale), out...  79.8 us
    convert_element_type x1, other arithmetic, on_device(): return (hidden, grad.astype(jnp.float32))  2.83 us

profile of v4, /device:TPU:24, one launch (start us, length us, event | category | flops | bytes accessed | tf_op | source)
XLA Modules:
  0.0 84.0 jit_solution(12696439780418081270)
XLA Ops:
  0.6 79.8 %shard_map.50 = (f32[128,512]{1,0:T(8,128)}, bf16[512,1024]{1,0:T(8,128)(2,1)}) custom-call(bf16[128,4096]{1,0:T(8,128)(2,1)} %tokens.1, bf16[512,1024]{1,0:T(8,128)(2,1)} %panel.1, bf16[128,512]{1,0:T(8,128)(2,1)} %cotangent.1), custom_call_target="tpu_custom_call" | custom-call | flops 2147483648 | bytes 2097152 | tf_op jit(solution)/shard_map/pallas_call | solution.py:308
  80.4 0.0 copy-start
  80.5 2.8 %convert_element_type.3 = f32[512,1024]{1,0:T(8,128)} convert(bf16[512,1024]{1,0:T(8,128)(2,1)} %get-tuple-element.5) | non-fusion elementwise | flops 524288 | bytes 3145728 | tf_op jit(solution)/shard_map/convert_element_type | solution.py:351
  83.3 0.0 copy-done
  83.3 0.7 copy.6
Async XLA Ops:
  80.4 2.8 %copy-start = (f32[128,512]{1,0:T(8,128)S(1)}, f32[128,512]{1,0:T(8,128)}, u32[]{:S(2)}) copy-start(f32[128,512]{1,0:T(8,128)} %get-tuple-element.8) | copy-start | bytes 786436

commit v5 on v4

--- a/solution.py
+++ b/solution.py
@@ -31,7 +31,7 @@
     hidden, grad,
     tok_v, ct_v, hid_v, stage, tok_x, tok_t, pan, mate_out, mate_in, sum_out, sum_in, own_part,
     proj, pre_all, row_own, row_out, row_in, team_in,
-    in_sem, own_s, pan_s, pan_r, tok_s, tok_r, mate_s, mate_r, sum_s, sum_r,
+    in_sem, pan_sem, own_s, pan_s, pan_r, tok_s, tok_r, mate_s, mate_r, sum_s, sum_r,
     pre_s, pre_r, pair_s, pair_r, row_s, row_r, team_s, team_r, ag_s, ag_r,
 ):
     n_tok, _ = tokens.shape
@@ -70,16 +70,27 @@
     def dp_of(i):
         return g * n_s + i
 
-    def part(p):
-        return pl.ds(p * width, width)
-
-    def pan_own(way):
+    units = cols // 2
+    half = width // 2
+
+    def columns(p, up):
+        return pl.ds(up * units + p * half, half)
+
+    def pan_in(p, up):
+        return pltpu.make_async_copy(
+            panel.at[slots(s, r), columns(p, up)],
+            pan.at[p, slots(z, r), pl.ds(up * half, half)],
+            pan_sem.at[p, up],
+        )
+
+    def pan_own(p, way):
+        ref = pan.at[p, slots(z, r)]
         to = (z + 2 * way - 1) * 2 + c
-        return send(panel.at[slots(s, r)], pan.at[slots(z, r)], own_s.at[way], pan_r.at[z], d, to)
-
-    def pan_on(src, to):
-        ref = pan.at[slots(src, r)]
-        return send(ref, ref, pan_s.at[src], pan_r.at[src], d, to * 2 + c)
+        return send(ref, ref, own_s.at[p, way], pan_r.at[p, z], d, to)
+
+    def pan_on(p, src, to):
+        ref = pan.at[p, slots(src, r)]
+        return send(ref, ref, pan_s.at[p, src], pan_r.at[p, src], d, to * 2 + c)
 
     my_slot = c * n_s + s
 
@@ -119,19 +130,20 @@
             ((g + k) % n_g) * n_s + s, t,
         )
 
-    def ag(p, j, owner):
-        ref = grad.at[slots(owner, r), part(p)]
-        return send(ref, ref, ag_s.at[p, j], ag_r.at[p, j], dp_of(mate(j)), t)
+    def ag(p, j, owner, up):
+        ref = grad.at[slots(owner, r), columns(p, up)]
+        return send(ref, ref, ag_s.at[p, j, up], ag_r.at[p, j, up], dp_of(mate(j)), t)
 
     def both_ways(copy, act):
         pl.when(z > 0)(lambda: act(copy(0)))
         pl.when(z < n_z - 1)(lambda: act(copy(1)))
 
+    for p in range(PARTS):
+        pan_in(p, 0).start()
+        pan_in(p, 1).start()
     tokens_in = pltpu.make_async_copy(tokens, tok_v, in_sem.at[0])
-    panel_in = pltpu.make_async_copy(panel.at[slots(s, r)], pan.at[slots(z, r)], in_sem.at[1])
-    ct_in = pltpu.make_async_copy(cotangent, ct_v, in_sem.at[2])
+    ct_in = pltpu.make_async_copy(cotangent, ct_v, in_sem.at[1])
     tokens_in.start()
-    panel_in.start()
     ct_in.start()
 
     barrier = pltpu.get_barrier_semaphore()
@@ -148,7 +160,12 @@
     repeat(1, n_g, lambda k: greet(((g + k) % n_g) * n_s + s, t))
     pl.semaphore_wait(barrier, n_z + 2 * n_s + n_g - 3)
 
-    both_ways(pan_own, lambda copy: copy.start())
+    def offer(p):
+        pan_in(p, 0).wait()
+        pan_in(p, 1).wait()
+        both_ways(lambda way: pan_own(p, way), lambda copy: copy.start())
+
+    offer(0)
     tokens_in.wait()
 
     for e in range(2 * n_s):
@@ -157,64 +174,76 @@
             stage[e, :, i * r:(i + 1) * r] = tok_v[:, first:first + r]
     repeat(1, 2 * n_s, lambda k: tok(k).start())
     tok_x[slots(my_slot, n_tok), :] = stage[my_slot]
-    tok_t[:, slots(my_slot, n_tok)] = stage[my_slot].T
-
-    def pass_on(n):
+    ct_in.wait()
+
+    def pass_on(p, n):
         src, to = arrival(n)
-        pan_on(src, to).wait_recv()
-        pl.when(inside(to))(lambda: pan_on(src, to).start())
+        pan_on(p, src, to).wait_recv()
+        pl.when(inside(to))(lambda: pan_on(p, src, to).start())
 
     def take(k):
-        e = (my_slot - k + 2 * n_s) % (2 * n_s)
-        ref = tok_x.at[slots(e, n_tok)]
+        ref = tok_x.at[slots((my_slot - k + 2 * n_s) % (2 * n_s), n_tok)]
         send(ref, ref, tok_s.at[k], tok_r.at[k], d, pair).wait_recv()
-        tok_t[:, slots(e, n_tok)] = ref[...].T
-
-    if n_z > 1:
-        pass_on(0)
-    repeat(1, n_s, take)
-    repeat(1, n_z - 2, pass_on)
-    repeat(n_s, 2 * n_s, take)
-    if n_z > 2:
-        pass_on(n_z - 2)
-    panel_in.wait()
-    ct_in.wait()
+
+    def transpose(e):
+        tok_t[:, slots(e, n_tok)] = tok_x[slots(e, n_tok), :].T
 
     team_rows = n_s * n_tok
-    for p in range(PARTS):
+
+    def partial(p):
         mate_out[p] = jnp.dot(
-            tok_x[slots(1 - c, team_rows), :], pan[:, part(p)], preferred_element_type=jnp.float32
+            tok_x[slots(1 - c, team_rows), :], pan[p], preferred_element_type=jnp.float32
         ).astype(jnp.bfloat16)
         halfway(p).start()
-    for p in range(PARTS):
         own_part[...] = jnp.dot(
-            tok_x[slots(c, team_rows), :], pan[:, part(p)], preferred_element_type=jnp.float32
+            tok_x[slots(c, team_rows), :], pan[p], preferred_element_type=jnp.float32
         )
         halfway(p).wait_recv()
         own_part[...] += mate_in[p].astype(jnp.float32)
         sum_out[p] = own_part[...].astype(jnp.bfloat16)
         repeat(1, n_s, lambda j: sums(p, j).start())
-        proj[:, part(p)] = own_part[slots(s, n_tok), :]
-    for p in range(PARTS):
+        proj[p] = own_part[slots(s, n_tok), :]
+
+    def activate(p):
         def add(j):
             sums(p, j).wait_recv()
-            proj[:, part(p)] += sum_in[p, j].astype(jnp.float32)
+            proj[p] += sum_in[p, j].astype(jnp.float32)
 
         repeat(1, n_s, add)
-
-    gate = proj[:, part(0)]
-    up = proj[:, part(1)]
-    sig = jax.nn.sigmoid(gate)
-    act = gate * sig
-    ct = ct_v[...].astype(jnp.float32)
-    pre_all[0, slots(my_slot, n_tok), :] = (ct * up * sig * (1.0 + gate * (1.0 - sig))).astype(jnp.bfloat16)
-    pre_all[1, slots(my_slot, n_tok), :] = (ct * act).astype(jnp.bfloat16)
-    for p in range(PARTS):
+        gate = proj[p, :, :half]
+        up = proj[p, :, half:]
+        sig = jax.nn.sigmoid(gate)
+        act = gate * sig
+        ct = ct_v[:, p * half:(p + 1) * half].astype(jnp.float32)
+        gate_grad = ct * up * sig * (1.0 + gate * (1.0 - sig))
+        pre_all[p, slots(my_slot, n_tok), :half] = gate_grad.astype(jnp.bfloat16)
+        pre_all[p, slots(my_slot, n_tok), half:] = (ct * act).astype(jnp.bfloat16)
         repeat(1, n_s, lambda j: pre(p, j, s).start())
         pre_pair(p, 0, c).start()
-    hid_v[...] = act * up
-    hidden_out = pltpu.make_async_copy(hid_v, hidden, in_sem.at[3])
-    hidden_out.start()
+        hid_v[:, p * half:(p + 1) * half] = act * up
+
+    def gather(p):
+        def arrive(j):
+            pre(p, j, mate(-j + n_s)).wait_recv()
+            pre_pair(p, j, c).start()
+
+        repeat(1, n_s, arrive)
+
+    def product(p, k):
+        to = (z + k) % n_z
+        return scale * jnp.dot(
+            tok_t[slots(to, r), :], pre_all[p], preferred_element_type=jnp.float32
+        )
+
+    def rows_out(p):
+        repeat(0, n_s, lambda j: pre_pair(p, j, 1 - c).wait_recv())
+
+        def product_out(k):
+            row_out[p, slots((z + k) % n_z, r), :] = product(p, k).astype(jnp.bfloat16)
+            rows_to(p, k).start()
+
+        repeat(1, n_z, product_out)
+        row_own[p] = product(p, 0)
 
     def finish(p):
         own_rows = row_own.at[p]
@@ -239,44 +268,49 @@
                 own_rows[...] += team_in[p, i].astype(jnp.float32)
 
             repeat(0, n_g, add_team)
-        grad[slots(s, r), part(p)] = own_rows[...].astype(jnp.bfloat16)
-        repeat(1, n_s, lambda j: ag(p, j, s).start())
-
+        for up in range(2):
+            grad[slots(s, r), columns(p, up)] = own_rows[:, up * half:(up + 1) * half].astype(jnp.bfloat16)
+            repeat(1, n_s, lambda j: ag(p, j, s, up).start())
+
+    hidden_out = pltpu.make_async_copy(hid_v, hidden, in_sem.at[2])
+
+    z_time, xy_time, sum_time = 16.0 / PARTS, 10.5 / PARTS, 21.0 / PARTS
+    plan = []
     for p in range(PARTS):
-        def arrive(j):
-            pre(p, j, mate(-j + n_s)).wait_recv()
-            pre_pair(p, j, c).start()
-
-        repeat(1, n_s, arrive)
-        repeat(0, n_s, lambda j: pre_pair(p, j, 1 - c).wait_recv())
-
-        def product(k):
-            to = (z + k) % n_z
-            return scale * jnp.dot(
-                tok_t[slots(to, r), :], pre_all[p], preferred_element_type=jnp.float32
-            )
-
-        def product_out(k):
-            row_out[p, slots((z + k) % n_z, r), :] = product(k).astype(jnp.bfloat16)
-            rows_to(p, k).start()
-
-        repeat(1, n_z, product_out)
-        row_own[p] = product(0)
+        for n in range(n_z - 1):
+            plan.append((z_time * (p + (n + 1) / (n_z - 1)) + 1.0 + n / n_z, functools.partial(pass_on, p, n)))
+            if n == 0 and p + 1 < PARTS:
+                plan.append((plan[-1][0] + 0.01, functools.partial(offer, p + 1)))
+        ready = z_time * (p + 1) + 2.0
+        plan.append((ready, functools.partial(partial, p)))
+        ready = max(ready + 3.0, 13.0 + xy_time * p) + xy_time
+        plan.append((ready, functools.partial(activate, p)))
+        ready = ready + 1.5 + xy_time
+        plan.append((ready, functools.partial(gather, p)))
+        ready = ready + 1.0
+        plan.append((ready, functools.partial(rows_out, p)))
+        ready = max(ready + 1.5, 27.0 + sum_time * p) + sum_time
+        plan.append((ready, functools.partial(finish, p)))
+    last_partial = z_time * PARTS + 2.0
+    plan.append((z_time + 1.99, lambda: repeat(1, 2 * n_s, take)))
+    plan.append((last_partial + 0.01, lambda: repeat(0, 2 * n_s, transpose)))
+    for _, run in sorted(plan, key=lambda item: item[0]):
+        run()
+    hidden_out.start()
     for p in range(PARTS):
-        finish(p)
-    for p in range(PARTS):
-        repeat(1, n_s, lambda j: ag(p, j, mate(-j + n_s)).wait_recv())
+        for up in range(2):
+            repeat(1, n_s, lambda j: ag(p, j, mate(-j + n_s), up).wait_recv())
 
     hidden_out.wait()
-    both_ways(pan_own, lambda copy: copy.wait_send())
-
-    def passed_on(n):
-        src, to = arrival(n)
-        pl.when(inside(to))(lambda: pan_on(src, to).wait_send())
-
-    repeat(0, n_z - 1, passed_on)
     repeat(1, 2 * n_s, lambda k: tok(k).wait_send())
     for p in range(PARTS):
+        both_ways(lambda way: pan_own(p, way), lambda copy: copy.wait_send())
+
+        def passed_on(n):
+            src, to = arrival(n)
+            pl.when(inside(to))(lambda: pan_on(p, src, to).wait_send())
+
+        repeat(0, n_z - 1, passed_on)
         halfway(p).wait_send()
         repeat(1, n_z, lambda k: rows_to(p, k).wait_send())
         repeat(1, n_g, lambda k: team(p, k).wait_send())
@@ -285,7 +319,8 @@
         def sent(j):
             sums(p, j).wait_send()
             pre(p, j, s).wait_send()
-            ag(p, j, s).wait_send()
+            ag(p, j, s, 0).wait_send()
+            ag(p, j, s, 1).wait_send()
 
         repeat(1, n_s, sent)
 
@@ -320,25 +355,26 @@
             pltpu.VMEM((2 * n_s, n_tok, n_z * r), bf16),
             pltpu.VMEM((2 * team, n_z * r), bf16),
             pltpu.VMEM((n_z * r, 2 * team), bf16),
-            pltpu.VMEM((n_z * r, cols), bf16),
+            pltpu.VMEM((PARTS, n_z * r, width), bf16),
             pltpu.VMEM((PARTS, team, width), bf16),
             pltpu.VMEM((PARTS, team, width), bf16),
             pltpu.VMEM((PARTS, team, width), bf16),
             pltpu.VMEM((PARTS, n_s, n_tok, width), bf16),
             pltpu.VMEM((team, width), f32),
-            pltpu.VMEM((n_tok, cols), f32),
+            pltpu.VMEM((PARTS, n_tok, width), f32),
             pltpu.VMEM((PARTS, 2 * team, width), bf16),
             pltpu.VMEM((PARTS, r, width), f32),
             pltpu.VMEM((PARTS, n_z * r, width), bf16),
             pltpu.VMEM((PARTS, n_z, r, width), bf16),
             pltpu.VMEM((PARTS, n_g, r, width), bf16),
         ]
-        + [dma((4,)), dma((2,)), dma((n_z,)), dma((n_z,)), dma((2 * n_s,)), dma((2 * n_s,))]
+        + [dma((3,)), dma((PARTS, 2)), dma((PARTS, 2)), dma((PARTS, n_z)), dma((PARTS, n_z))]
+        + [dma((2 * n_s,))] * 2
         + [dma((PARTS,))] * 2
         + [dma((PARTS, n_s))] * 6
         + [dma((PARTS, n_z))] * 2
         + [dma((PARTS, n_g))] * 2
-        + [dma((PARTS, n_s))] * 2,
+        + [dma((PARTS, n_s, 2))] * 2,
         compiler_params=pltpu.CompilerParams(
             collective_id=0, has_side_effects=True, vmem_limit_bytes=60 * 1024 * 1024
         ),

time: 84.2 us -> 81.2 us (0.964)
  Pallas kernels: 79.8 us -> 76.9 us
    pallas_call x1, Pallas kernels: 79.8 us -> 76.9 us  [on_device(): pl.pallas_call(functools.partial(kernel, n_dp, n_tensor, n_s, scale), out...]
where the time goes in v5:
time: 81.2 us; the launch traced here: 81 us
  Pallas kernels  76.9 us (95%)
  other arithmetic  2.83 us (3%)
    pallas_call x1, Pallas kernels, on_device(): pl.pallas_call(functools.partial(kernel, n_dp, n_tensor, n_s, scale), out...  76.9 us
    convert_element_type x1, other arithmetic, on_device(): return (hidden, grad.astype(jnp.float32))  2.83 us

profile of v5, /device:TPU:24, one launch (start us, length us, event | category | flops | bytes accessed | tf_op | source)
XLA Modules:
  0.0 81.0 jit_solution(851440614858311195)
XLA Ops:
  0.6 76.9 %shard_map.50 = (f32[128,512]{1,0:T(8,128)}, bf16[512,1024]{1,0:T(8,128)(2,1)}) custom-call(bf16[128,4096]{1,0:T(8,128)(2,1)} %tokens.1, bf16[512,1024]{1,0:T(8,128)(2,1)} %panel.1, bf16[128,512]{1,0:T(8,128)(2,1)} %cotangent.1), custom_call_target="tpu_custom_call" | custom-call | flops 2147483648 | bytes 2097152 | tf_op jit(solution)/shard_map/pallas_call | solution.py:343
  77.5 0.0 copy-start
  77.5 2.8 %convert_element_type.3 = f32[512,1024]{1,0:T(8,128)} convert(bf16[512,1024]{1,0:T(8,128)(2,1)} %get-tuple-element.5) | non-fusion elementwise | flops 524288 | bytes 3145728 | tf_op jit(solution)/shard_map/convert_element_type | solution.py:387
  80.3 0.0 copy-done
  80.3 0.7 copy.6
Async XLA Ops:
  77.5 2.8 %copy-start = (f32[128,512]{1,0:T(8,128)S(1)}, f32[128,512]{1,0:T(8,128)}, u32[]{:S(2)}) copy-start(f32[128,512]{1,0:T(8,128)} %get-tuple-element.8) | copy-start | bytes 786436

commit v6 on v5

--- a/solution.py
+++ b/solution.py
@@ -14,7 +14,7 @@
 
 
 def repeat(low, high, body):
-    if high - low <= 4:
+    if high - low <= 1:
         for i in range(low, high):
             body(i)
     else:
@@ -188,20 +188,36 @@
     def transpose(e):
         tok_t[:, slots(e, n_tok)] = tok_x[slots(e, n_tok), :].T
 
-    team_rows = n_s * n_tok
+    tile = n_tok * max(i for i in (1, 2) if n_s % i == 0)
+    tiles = n_s * n_tok // tile
 
     def partial(p):
-        mate_out[p] = jnp.dot(
-            tok_x[slots(1 - c, team_rows), :], pan[p], preferred_element_type=jnp.float32
-        ).astype(jnp.bfloat16)
-        halfway(p).start()
-        own_part[...] = jnp.dot(
-            tok_x[slots(c, team_rows), :], pan[p], preferred_element_type=jnp.float32
-        )
+        def one(i):
+            core = lax.rem(i // tiles + 1 + c, 2)
+            rows = slots(i % tiles, tile)
+            own_part[rows, :] = jnp.dot(
+                tok_x[slots(core * tiles + i % tiles, tile), :], pan[p],
+                preferred_element_type=jnp.float32,
+            )
+
+            @pl.when(i < tiles)
+            def _():
+                mate_out[p, rows, :] = own_part[rows, :].astype(jnp.bfloat16)
+
+            @pl.when(i == tiles - 1)
+            def _():
+                halfway(p).start()
+
+        repeat(0, 2 * tiles, one)
         halfway(p).wait_recv()
-        own_part[...] += mate_in[p].astype(jnp.float32)
-        sum_out[p] = own_part[...].astype(jnp.bfloat16)
-        repeat(1, n_s, lambda j: sums(p, j).start())
+
+        def add(j):
+            rows = slots(mate(j), n_tok)
+            own_part[rows, :] += mate_in[p, rows, :].astype(jnp.float32)
+            sum_out[p, rows, :] = own_part[rows, :].astype(jnp.bfloat16)
+            pl.when(j < n_s)(lambda: sums(p, j).start())
+
+        repeat(1, n_s + 1, add)
         proj[p] = own_part[slots(s, n_tok), :]
 
     def activate(p):
@@ -240,13 +256,13 @@
 
         def product_out(k):
             row_out[p, slots((z + k) % n_z, r), :] = product(p, k).astype(jnp.bfloat16)
-            rows_to(p, k).start()
-
-        repeat(1, n_z, product_out)
-        row_own[p] = product(p, 0)
+            pl.when(k < n_z)(lambda: rows_to(p, k).start())
+
+        repeat(1, n_z + 1, product_out)
 
     def finish(p):
         own_rows = row_own.at[p]
+        own_rows[...] = row_out[p, slots(z, r), :].astype(jnp.float32)
 
         def add(k):
             rows_to(p, k).wait_recv()

time: 81.2 us -> 81.6 us (level)
  no operation moved by 1% of the time
where the time goes in v6:
time: 81.6 us; the launch traced here: 81.5 us
  Pallas kernels  77.3 us (95%)
  other arithmetic  2.83 us (3%)
    pallas_call x1, Pallas kernels, on_device(): pl.pallas_call(functools.partial(kernel, n_dp, n_tensor, n_s, scale), out...  77.3 us
    convert_element_type x1, other arithmetic, on_device(): return (hidden, grad.astype(jnp.float32))  2.83 us

profile of v6, /device:TPU:24, one launch (start us, length us, event | category | flops | bytes accessed | tf_op | source)
XLA Modules:
  0.0 81.5 jit_solution(11087552215941707751)
XLA Ops:
  0.6 77.3 %shard_map.50 = (f32[128,512]{1,0:T(8,128)}, bf16[512,1024]{1,0:T(8,128)(2,1)}) custom-call(bf16[128,4096]{1,0:T(8,128)(2,1)} %tokens.1, bf16[512,1024]{1,0:T(8,128)(2,1)} %panel.1, bf16[128,512]{1,0:T(8,128)(2,1)} %cotangent.1), custom_call_target="tpu_custom_call" | custom-call | flops 2147483648 | bytes 2097152 | tf_op jit(solution)/shard_map/pallas_call | solution.py:359
  77.9 0.0 copy-start
  78.0 2.8 %convert_element_type.3 = f32[512,1024]{1,0:T(8,128)} convert(bf16[512,1024]{1,0:T(8,128)(2,1)} %get-tuple-element.5) | non-fusion elementwise | flops 524288 | bytes 3145728 | tf_op jit(solution)/shard_map/convert_element_type | solution.py:403
  80.8 0.0 copy-done
  80.8 0.7 copy.6
Async XLA Ops:
  77.9 2.8 %copy-start = (f32[128,512]{1,0:T(8,128)S(1)}, f32[128,512]{1,0:T(8,128)}, u32[]{:S(2)}) copy-start(f32[128,512]{1,0:T(8,128)} %get-tuple-element.8) | copy-start | bytes 786436

commit v7 on v6

--- a/solution.py
+++ b/solution.py
@@ -31,7 +31,7 @@
     hidden, grad,
     tok_v, ct_v, hid_v, stage, tok_x, tok_t, pan, mate_out, mate_in, sum_out, sum_in, own_part,
     proj, pre_all, row_own, row_out, row_in, team_in,
-    in_sem, pan_sem, own_s, pan_s, pan_r, tok_s, tok_r, mate_s, mate_r, sum_s, sum_r,
+    in_sem, pan_sem, pan_s, pan_r, tok_s, tok_r, mate_s, mate_r, sum_s, sum_r,
     pre_s, pre_r, pair_s, pair_r, row_s, row_r, team_s, team_r, ag_s, ag_r,
 ):
     n_tok, _ = tokens.shape
@@ -51,16 +51,6 @@
             device_id=(dp, tensor), device_id_type=MESH,
         )
 
-    def arrival(n):
-        short = jnp.minimum(z, n_z - 1 - z)
-        both = n < 2 * short
-        m = jnp.where(both, n // 2 + 1, n - short + 1)
-        side = jnp.where(both, 2 * (n % 2) - 1, jnp.where(z > n_z - 1 - z, -1, 1))
-        return z + side * m, z - side
-
-    def inside(place):
-        return (place >= 0) & (place < n_z)
-
     def slots(i, size):
         return pl.ds(pl.multiple_of(i * size, size), size)
 
@@ -83,14 +73,13 @@
             pan_sem.at[p, up],
         )
 
-    def pan_own(p, way):
+    def pan_to(p, k):
         ref = pan.at[p, slots(z, r)]
-        to = (z + 2 * way - 1) * 2 + c
-        return send(ref, ref, own_s.at[p, way], pan_r.at[p, z], d, to)
-
-    def pan_on(p, src, to):
-        ref = pan.at[p, slots(src, r)]
-        return send(ref, ref, pan_s.at[p, src], pan_r.at[p, src], d, to * 2 + c)
+        return send(ref, ref, pan_s.at[p, k], pan_r.at[p, k], d, ((z + k) % n_z) * 2 + c)
+
+    def pan_from(p, k):
+        ref = pan.at[p, slots((z - k + n_z) % n_z, r)]
+        return send(ref, ref, pan_s.at[p, k], pan_r.at[p, k], d, pair)
 
     my_slot = c * n_s + s
 
@@ -133,10 +122,6 @@
     def ag(p, j, owner, up):
         ref = grad.at[slots(owner, r), columns(p, up)]
         return send(ref, ref, ag_s.at[p, j, up], ag_r.at[p, j, up], dp_of(mate(j)), t)
-
-    def both_ways(copy, act):
-        pl.when(z > 0)(lambda: act(copy(0)))
-        pl.when(z < n_z - 1)(lambda: act(copy(1)))
 
     for p in range(PARTS):
         pan_in(p, 0).start()
@@ -163,7 +148,7 @@
     def offer(p):
         pan_in(p, 0).wait()
         pan_in(p, 1).wait()
-        both_ways(lambda way: pan_own(p, way), lambda copy: copy.start())
+        repeat(1, n_z, lambda k: pan_to(p, k).start())
 
     offer(0)
     tokens_in.wait()
@@ -176,10 +161,8 @@
     tok_x[slots(my_slot, n_tok), :] = stage[my_slot]
     ct_in.wait()
 
-    def pass_on(p, n):
-        src, to = arrival(n)
-        pan_on(p, src, to).wait_recv()
-        pl.when(inside(to))(lambda: pan_on(p, src, to).start())
+    def collect(p, low, high):
+        repeat(low, high, lambda k: pan_from(p, k).wait_recv())
 
     def take(k):
         ref = tok_x.at[slots((my_slot - k + 2 * n_s) % (2 * n_s), n_tok)]
@@ -290,13 +273,13 @@
 
     hidden_out = pltpu.make_async_copy(hid_v, hidden, in_sem.at[2])
 
-    z_time, xy_time, sum_time = 16.0 / PARTS, 10.5 / PARTS, 21.0 / PARTS
+    z_time, xy_time, sum_time = 21.0 / PARTS, 10.5 / PARTS, 21.0 / PARTS
     plan = []
     for p in range(PARTS):
-        for n in range(n_z - 1):
-            plan.append((z_time * (p + (n + 1) / (n_z - 1)) + 1.0 + n / n_z, functools.partial(pass_on, p, n)))
-            if n == 0 and p + 1 < PARTS:
-                plan.append((plan[-1][0] + 0.01, functools.partial(offer, p + 1)))
+        plan.append((z_time * (p + 0.4), functools.partial(collect, p, 1, 2)))
+        if p + 1 < PARTS:
+            plan.append((z_time * (p + 0.41), functools.partial(offer, p + 1)))
+        plan.append((z_time * (p + 1) + 1.0, functools.partial(collect, p, 2, n_z)))
         ready = z_time * (p + 1) + 2.0
         plan.append((ready, functools.partial(partial, p)))
         ready = max(ready + 3.0, 13.0 + xy_time * p) + xy_time
@@ -305,7 +288,7 @@
         plan.append((ready, functools.partial(gather, p)))
         ready = ready + 1.0
         plan.append((ready, functools.partial(rows_out, p)))
-        ready = max(ready + 1.5, 27.0 + sum_time * p) + sum_time
+        ready = max(ready + 1.5, 30.0 + sum_time * p) + sum_time
         plan.append((ready, functools.partial(finish, p)))
     last_partial = z_time * PARTS + 2.0
     plan.append((z_time + 1.99, lambda: repeat(1, 2 * n_s, take)))
@@ -320,13 +303,7 @@
     hidden_out.wait()
     repeat(1, 2 * n_s, lambda k: tok(k).wait_send())
     for p in range(PARTS):
-        both_ways(lambda way: pan_own(p, way), lambda copy: copy.wait_send())
-
-        def passed_on(n):
-            src, to = arrival(n)
-            pl.when(inside(to))(lambda: pan_on(p, src, to).wait_send())
-
-        repeat(0, n_z - 1, passed_on)
+        repeat(1, n_z, lambda k: pan_to(p, k).wait_send())
         halfway(p).wait_send()
         repeat(1, n_z, lambda k: rows_to(p, k).wait_send())
         repeat(1, n_g, lambda k: team(p, k).wait_send())
@@ -384,7 +361,7 @@
             pltpu.VMEM((PARTS, n_z, r, width), bf16),
             pltpu.VMEM((PARTS, n_g, r, width), bf16),
         ]
-        + [dma((3,)), dma((PARTS, 2)), dma((PARTS, 2)), dma((PARTS, n_z)), dma((PARTS, n_z))]
+        + [dma((3,)), dma((PARTS, 2)), dma((PARTS, n_z)), dma((PARTS, n_z))]
         + [dma((2 * n_s,))] * 2
         + [dma((PARTS,))] * 2
         + [dma((PARTS, n_s))] * 6

time: 81.6 us -> 79.3 us (0.972)
  Pallas kernels: 77.3 us -> 74.9 us
    pallas_call x1, Pallas kernels: 77.3 us -> 74.9 us  [on_device(): pl.pallas_call(functools.partial(kernel, n_dp, n_tensor, n_s, scale), out...]
where the time goes in v7:
time: 79.3 us; the launch traced here: 79.1 us
  Pallas kernels  74.9 us (94%)
  other arithmetic  2.83 us (4%)
    pallas_call x1, Pallas kernels, on_device(): pl.pallas_call(functools.partial(kernel, n_dp, n_tensor, n_s, scale), out...  74.9 us
    convert_element_type x1, other arithmetic, on_device(): return (hidden, grad.astype(jnp.float32))  2.83 us

profile of v7, /device:TPU:24, one launch (start us, length us, event | category | flops | bytes accessed | tf_op | source)
XLA Modules:
  0.0 79.1 jit_solution(13922401642652875966)
XLA Ops:
  0.6 74.9 %shard_map.50 = (f32[128,512]{1,0:T(8,128)}, bf16[512,1024]{1,0:T(8,128)(2,1)}) custom-call(bf16[128,4096]{1,0:T(8,128)(2,1)} %tokens.1, bf16[512,1024]{1,0:T(8,128)(2,1)} %panel.1, bf16[128,512]{1,0:T(8,128)(2,1)} %cotangent.1), custom_call_target="tpu_custom_call" | custom-call | flops 2147483648 | bytes 2097152 | tf_op jit(solution)/shard_map/pallas_call | solution.py:336
  75.5 0.0 copy-start
  75.5 2.8 %convert_element_type.3 = f32[512,1024]{1,0:T(8,128)} convert(bf16[512,1024]{1,0:T(8,128)(2,1)} %get-tuple-element.5) | non-fusion elementwise | flops 524288 | bytes 3145728 | tf_op jit(solution)/shard_map/convert_element_type | solution.py:380
  78.4 0.0 copy-done
  78.4 0.7 copy.6
Async XLA Ops:
  75.5 2.8 %copy-start = (f32[128,512]{1,0:T(8,128)S(1)}, f32[128,512]{1,0:T(8,128)}, u32[]{:S(2)}) copy-start(f32[128,512]{1,0:T(8,128)} %get-tuple-element.8) | copy-start | bytes 786436

commit v8 on v7

--- a/solution.py
+++ b/solution.py
@@ -9,7 +9,7 @@
 from jax.sharding import PartitionSpec as P
 
 MESH = pl.DeviceIdType.MESH
-PARTS = 2
+PARTS = 4
 LANES = 128
 
 
@@ -290,9 +290,8 @@
         plan.append((ready, functools.partial(rows_out, p)))
         ready = max(ready + 1.5, 30.0 + sum_time * p) + sum_time
         plan.append((ready, functools.partial(finish, p)))
-    last_partial = z_time * PARTS + 2.0
     plan.append((z_time + 1.99, lambda: repeat(1, 2 * n_s, take)))
-    plan.append((last_partial + 0.01, lambda: repeat(0, 2 * n_s, transpose)))
+    plan.append((z_time + 2.01, lambda: repeat(0, 2 * n_s, transpose)))
     for _, run in sorted(plan, key=lambda item: item[0]):
         run()
     hidden_out.start()

time: 79.3 us -> 79.8 us (level)
  the two profiles are of different devices: /device:TPU:24 before, /device:TPU:8 now
where the time goes in v8:
time: 79.8 us; the launch traced here: 79.7 us
  Pallas kernels  75.5 us (95%)
  other arithmetic  2.83 us (4%)
    pallas_call x1, Pallas kernels, on_device(): pl.pallas_call(functools.partial(kernel, n_dp, n_tensor, n_s, scale), out...  75.5 us
    convert_element_type x1, other arithmetic, on_device(): return (hidden, grad.astype(jnp.float32))  2.83 us

profile of v8, /device:TPU:8, one launch (start us, length us, event | category | flops | bytes accessed | tf_op | source)
XLA Modules:
  0.0 79.7 jit_solution(12481476856441306474)
XLA Ops:
  0.6 75.5 %shard_map.50 = (f32[128,512]{1,0:T(8,128)}, bf16[512,1024]{1,0:T(8,128)(2,1)}) custom-call(bf16[128,4096]{1,0:T(8,128)(2,1)} %tokens.1, bf16[512,1024]{1,0:T(8,128)(2,1)} %panel.1, bf16[128,512]{1,0:T(8,128)(2,1)} %cotangent.1), custom_call_target="tpu_custom_call" | custom-call | flops 2147483648 | bytes 2097152 | tf_op jit(solution)/shard_map/pallas_call | solution.py:335
  76.1 0.0 copy-start
  76.1 2.8 %convert_element_type.3 = f32[512,1024]{1,0:T(8,128)} convert(bf16[512,1024]{1,0:T(8,128)(2,1)} %get-tuple-element.5) | non-fusion elementwise | flops 524288 | bytes 3145728 | tf_op jit(solution)/shard_map/convert_element_type | solution.py:379
  79.0 0.0 copy-done
  79.0 0.7 copy.6
Async XLA Ops:
  76.1 2.8 %copy-start = (f32[128,512]{1,0:T(8,128)S(1)}, f32[128,512]{1,0:T(8,128)}, u32[]{:S(2)}) copy-start(f32[128,512]{1,0:T(8,128)} %get-tuple-element.8) | copy-start | bytes 786436
